TPU v7x, 512 devices: a whole 4x8x8 slice. The times are simulated.
512 devices in a mesh: pos: 64 (over y, z_lo, core), off: 8 (over z_hi, x).
Axes of the slice: x: 4, y: 8, z: 8 (z_hi: 2, z_lo: 4; z = z_hi * 4 + z_lo), core: 2. Of those that a mesh axis runs over, the one named last changes fastest.
Arguments:
- counts: float32 [16384, 8192], P('pos', 'off'), as said below
- bin_mask: int32 [16384], P('pos'), may hold values 0 or 1
Outputs:
- donut_enrich: float32 [16384, 8192], P('pos', 'off')
- lower_enrich: float32 [16384, 8192], P('pos', 'off')
Inputs may be any that keep to these rules, and one draw needn't show every extreme that they name: `counts`: every entry is a nonnegative whole number.
All inputs are finite; a program needn't handle non-finite values. No bound on the sum of `bin_mask` on one device may be relied on, other than what follows from the above.
Results may differ from a plain program's by a relative error of at most 0.00075.
Values sent between devices are 32-bit elements; how exact they have to be, the bound alone decides.
A program may use at most 64 MiB of HBM per device.

v0:
```python
import jax
import jax.numpy as jnp
from jax import lax
from jax.sharding import PartitionSpec as P

W = 20
P_SIZE = 8


def padded(cells, sides, width):
    for axis, dim in sides:
        count = lax.axis_size(axis)
        ends = count - 1
        head = lax.slice_in_dim(cells, 0, width, axis=dim)
        tail = lax.slice_in_dim(cells, cells.shape[dim] - width, cells.shape[dim], axis=dim)
        cells = jnp.concatenate(
            [
                lax.ppermute(tail, axis, [(i, (i + 1) % count) for i in range(ends)]),
                cells,
                lax.ppermute(head, axis, [((i + 1) % count, i) for i in range(ends)]),
            ],
            axis=dim,
        )
    return cells


def hankel_rows(segment, row_count, col_count):
    length = segment.shape[0]
    repeated = jnp.tile(segment, row_count + 1)
    framed = repeated[: row_count * (length + 1)].reshape(row_count, length + 1)
    return framed[:, :col_count]


def band_table(cols_in, cols_out, margin, lowest, highest):
    column = lax.broadcasted_iota(jnp.int32, (cols_in, cols_out), 0)
    target = lax.broadcasted_iota(jnp.int32, (cols_in, cols_out), 1)
    distance = column - target - margin
    return ((distance >= lowest) & (distance <= highest)).astype(jnp.float32)


def factor_of(expected, pair_count):
    return pair_count / jnp.where(expected > 0, expected, jnp.ones_like(expected))


def local(counts, bin_mask):
    rows_dev, offs_dev = counts.shape
    total_bins = rows_dev * lax.axis_size("pos")
    band_width = offs_dev * lax.axis_size("off")
    first_row = lax.axis_index("pos") * rows_dev
    first_off = lax.axis_index("off") * offs_dev
    row_bins = first_row + lax.broadcasted_iota(jnp.int32, (rows_dev, offs_dev), 0)
    offsets = first_off + lax.broadcasted_iota(jnp.int32, (rows_dev, offs_dev), 1)
    kept_counts = jnp.where(row_bins + offsets < total_bins, counts, jnp.zeros_like(counts))
    coverage = lax.psum(jnp.sum(kept_counts, axis=1), "off")
    weight = bin_mask.astype(jnp.float32) / jnp.sqrt(coverage)
    weight_all = lax.all_gather(weight, "pos", axis=0, tiled=True)
    margin = 2 * W
    padded_weight = jnp.concatenate(
        [
            jnp.zeros((2 * margin,), jnp.float32),
            weight_all,
            jnp.zeros((band_width + rows_dev + 4 * margin,), jnp.float32),
        ]
    )
    row_count, col_count = kept_counts.shape
    row_weight = lax.dynamic_slice_in_dim(padded_weight, first_row + 2 * margin, row_count)
    segment = lax.dynamic_slice_in_dim(
        padded_weight, first_row + first_off + 2 * margin, row_count + col_count
    )
    col_weight = hankel_rows(segment, row_count, col_count)
    normed = kept_counts * row_weight[:, None] * col_weight
    live_pairs = ((row_weight[:, None] > 0) & (col_weight > 0)).astype(jnp.float32)
    normed, live_pairs = (normed, live_pairs)
    expected, pair_count = lax.psum((jnp.sum(normed, axis=0), jnp.sum(live_pairs, axis=0)), "pos")
    ratios = normed * factor_of(expected, pair_count)[None, :]
    wide_cols = padded(ratios, (("off", 1),), 2 * W)
    rows_block = padded(wide_cols, (("pos", 0),), W)
    cols_in = offs_dev + 4 * W
    cols_out = offs_dev + 2 * W

    def band_sum(lowest, highest):
        table = band_table(cols_in, cols_out, W, lowest, highest)
        return jnp.dot(
            rows_block, table, precision=lax.Precision.HIGHEST, preferred_element_type=jnp.float32
        )

    wide_box = band_sum(-W, W)
    peak_box = band_sum(-P_SIZE, P_SIZE)
    left_wide = band_sum(-W, -1)
    left_peak = band_sum(-P_SIZE, -1)
    donut_sum = jnp.zeros((rows_dev, offs_dev), jnp.float32)
    lower_sum = jnp.zeros((rows_dev, offs_dev), jnp.float32)
    for displace in range(-W, W + 1):
        row_sel = slice(W + displace, W + displace + rows_dev)
        col_sel = slice(W - displace, W - displace + offs_dev)
        if displace != 0:
            if abs(displace) <= P_SIZE:
                donut_sum = donut_sum + (wide_box[row_sel, col_sel] - peak_box[row_sel, col_sel])
            else:
                center = rows_block[row_sel, 2 * W - displace : 2 * W - displace + offs_dev]
                donut_sum = donut_sum + (wide_box[row_sel, col_sel] - center)
        if displace > 0:
            addend = left_wide[row_sel, col_sel]
            if displace <= P_SIZE:
                addend = addend - left_peak[row_sel, col_sel]
            lower_sum = lower_sum + addend
    ratios_here = rows_block[W : W + rows_dev, 2 * W : 2 * W + offs_dev]
    donut_cells = (2 * W + 1) ** 2 - (2 * P_SIZE + 1) ** 2 - 4 * (W - P_SIZE)
    lower_cells = W * W - P_SIZE * P_SIZE
    donut_enrich = ratios_here / jnp.maximum(donut_sum / donut_cells, 0.25)
    lower_enrich = ratios_here / jnp.maximum(lower_sum / lower_cells, 0.25)
    return (donut_enrich, lower_enrich)


def solution(mesh):
    placed = (P("pos", "off"), P("pos"))
    return jax.shard_map(
        local,
        mesh=mesh,
        in_specs=placed,
        out_specs=(P("pos", "off"), P("pos", "off")),
        check_vma=False,
    )
```

profile of v0, /device:TPU:38, one launch (start us, length us, event | category | flops | bytes accessed | tf_op | source)
XLA Modules:
  0.0 358.3 jit_solution(18333961616012391195)
XLA Ops:
  0.7 1.5 fusion.130
  2.2 26.7 %psum.21 = f32[256]{0:T(256)S(1)} all-reduce(f32[256]{0:T(256)S(1)} %fusion.130), channel_id=1, replica_groups=mesh['pos'=64,'off'=8] {'off'}, use_global_device_ids=true, to_apply=%region_1.2 | all-reduce | flops 256 | bytes 2048 | tf_op jit(solution)/shard_map/psum | solution.py:54
  28.8 0.7 rsqrt_multiply_fusion
  29.5 76.8 %all-gather = f32[64,1,256]{2,1,0:T(1,128)S(1)} all-gather(f32[1,1,256]{2,1,0:T(1,128)S(1)} %bitcast.3), channel_id=1, replica_groups=mesh['pos'=64,'off'=8] {'pos'}, dimensions={0}, use_global_device_ids=true | all-gather | bytes 66560 | tf_op jit(solution)/shard_map/all_gather | solution.py:56
  106.4 0.1 concatenate.37
  106.5 0.0 copy-start.3
  106.5 0.6 copy-done.3
  107.1 0.1 dynamic_slice.7
  107.2 0.1 tile.4
  107.3 0.1 tile.10
  107.4 1.1 slice.480
  108.5 0.0 copy-start.1
  108.6 2.5 reshape.12
  111.1 0.8 broadcast_compare_fusion
  111.9 0.0 copy-done.1
  111.9 0.4 fusion.146
  112.3 136.0 %all-reduce = (f32[1024]{0:T(1024)S(1)}, f32[1024]{0:T(1024)S(1)}) all-reduce(f32[1024]{0:T(1024)S(1)} %get-tuple-element.3, f32[1024]{0:T(1024)S(1)} %get-tuple-element.2), channel_id=1, replica_groups=mesh['pos'=64,'off'=8] {'pos'}, use_global_device_ids=true, to_apply=%region_3.4 | all-reduce | flops 2048 | bytes 16384 | tf_op jit(solution)/shard_map/psum | solution.py:74
  248.3 0.3 broadcast_multiply_fusion
  248.6 0.0 copy-start
  248.7 0.1 fusion.148
  248.8 9.7 %collective-permute-start = (f32[256,40]{1,0:T(8,128)S(1)}, f32[256,40]{1,0:T(8,128)S(1)}, u32[]{:S(2)}, u32[]{:S(2)}) collective-permute-start(f32[256,40]{1,0:T(8,128)S(1)} %get-tuple-element.11), channel_id=1, source_target_pairs={{0,1},{1,2},{2,3},{3,4},{4,5},{5,6},{6,7},{8,9},{9,10},{10,11},{11... | collective-permute-start | bytes 122888 | tf_op jit(solution)/shard_map/ppermute | solution.py:18
  258.4 1.9 collective-permute-start.1
  260.4 0.6 collective-permute-done
  260.9 10.4 %collective-permute-done.1 = f32[256,40]{1,0:T(8,128)S(1)} collective-permute-done((f32[256,40]{1,0:T(8,128)S(1)}, f32[256,40]{1,0:T(8,128)S(1)}, u32[]{:S(2)}, u32[]{:S(2)}) %collective-permute-start.1) | collective-permute-done | bytes 40992 | tf_op jit(solution)/shard_map/ppermute | solution.py:20
  271.3 0.7 concatenate.38
  272.0 0.0 copy-start.2
  272.1 1.9 collective-permute-start.2
  274.0 7.5 %collective-permute-start.3 = (f32[20,1104]{1,0:T(8,128)S(1)}, f32[20,1104]{1,0:T(8,128)S(1)}, u32[]{:S(2)}, u32[]{:S(2)}) collective-permute-start(f32[20,1104]{1,0:T(8,128)S(1)} %get-tuple-element.9), channel_id=1, source_target_pairs={{8,0},{16,8},{24,16},{32,24},{40,32},{48,40},{56,48},{64,56},{72,6... | collective-permute-start | bytes 264968 | tf_op jit(solution)/shard_map/ppermute | solution.py:20
  281.5 0.5 collective-permute-done.2
  282.0 1.8 collective-permute-done.3
  283.9 3.2 fusion.7
  287.1 3.3 fusion.9
  290.4 0.0 copy-done
  290.4 10.4 %fusion.119 = f32[256,1024]{1,0:T(8,128)} fusion(f32[256,1024]{1,0:T(8,128)S(1)} %broadcast_multiply_fusion, f32[296,1064]{1,0:T(8,128)S(1)} %fusion.9, f32[296,1064]{1,0:T(8,128)S(1)} %fusion.7), kind=kLoop, calls=%fused_computation.158 | loop fusion | flops 7864320 | bytes 31457280 | tf_op jit(solution)/shard_map/div | solution.py:111
  300.8 0.0 copy-done.2
  300.8 3.2 fusion.11
  304.0 4.5 %fusion.13 = f32[296,1064]{1,0:T(8,128)S(1)} fusion(f32[20,1104]{1,0:T(8,128)S(1)} %collective-permute-done.3, f32[256,1104]{1,0:T(8,128)} %copy-done.2, f32[20,1104]{1,0:T(8,128)S(1)} %collective-permute-done.2), kind=kOutput, calls=%fused_computation.35 | convolution fusion | flops 4178905088 | bytes 2566912 | tf_op jit(solution)/shard_map/dot_general | solution.py:83
  308.5 49.6 %fusion.37 = f32[256,1024]{1,0:T(8,128)} fusion(f32[256,1024]{1,0:T(8,128)} %copy-done, f32[256,1104]{1,0:T(8,128)} %copy-done.2, f32[20,1104]{1,0:T(8,128)S(1)} %collective-permute-done.3, f32[20,1104]{1,0:T(8,128)S(1)} %collective-permute-done.2, f32[296,1064]{1,0:T(8,128)S(1)} %fusion.13, f32[296,1064]{1,0:T(8,128)S(1)} %fusion.11), kind=kLoop, calls=%fused_computation.75 | loop fusion | flops 27787264 | bytes 62124544 | tf_op jit(solution)/shard_map/div | solution.py:110
  (6 shorter events, 0.0 us)
Async XLA Ops:
  106.5 0.6 copy-start.3
  108.5 3.3 copy-start.1
  248.6 41.7 %copy-start = (f32[256,1024]{1,0:T(8,128)}, f32[256,1024]{1,0:T(8,128)S(1)}, u32[]{:S(2)}) copy-start(f32[256,1024]{1,0:T(8,128)S(1)} %broadcast_multiply_fusion) | copy-start | bytes 3145732
  248.8 12.2 %collective-permute-start = (f32[256,40]{1,0:T(8,128)S(1)}, f32[256,40]{1,0:T(8,128)S(1)}, u32[]{:S(2)}, u32[]{:S(2)}) collective-permute-start(f32[256,40]{1,0:T(8,128)S(1)} %get-tuple-element.11), channel_id=1, source_target_pairs={{0,1},{1,2},{2,3},{3,4},{4,5},{5,6},{6,7},{8,9},{9,10},{10,11},{11... | collective-permute-start | bytes 122888 | tf_op jit(solution)/shard_map/ppermute | solution.py:18
  258.4 12.9 %collective-permute-start.1 = (f32[256,40]{1,0:T(8,128)S(1)}, f32[256,40]{1,0:T(8,128)S(1)}, u32[]{:S(2)}, u32[]{:S(2)}) collective-permute-start(f32[256,40]{1,0:T(8,128)S(1)} %get-tuple-element.10), channel_id=1, source_target_pairs={{1,0},{2,1},{3,2},{4,3},{5,4},{6,5},{7,6},{9,8},{10,9},{11,10},{12... | collective-permute-start | bytes 122888 | tf_op jit(solution)/shard_map/ppermute | solution.py:20
  272.0 28.8 %copy-start.2 = (f32[256,1104]{1,0:T(8,128)}, f32[256,1104]{1,0:T(8,128)S(1)}, u32[]{:S(2)}) copy-start(f32[256,1104]{1,0:T(8,128)S(1)} %concatenate.38) | copy-start | bytes 3391492
  272.1 10.0 %collective-permute-start.2 = (f32[20,1104]{1,0:T(8,128)S(1)}, f32[20,1104]{1,0:T(8,128)S(1)}, u32[]{:S(2)}, u32[]{:S(2)}) collective-permute-start(f32[20,1104]{1,0:T(8,128)S(1)} %get-tuple-element.8), channel_id=1, source_target_pairs={{0,8},{8,16},{16,24},{24,32},{32,40},{40,48},{48,56},{56,64},{64,7... | collective-permute-start | bytes 264968 | tf_op jit(solution)/shard_map/ppermute | solution.py:18
  274.0 9.9 %collective-permute-start.3 = (f32[20,1104]{1,0:T(8,128)S(1)}, f32[20,1104]{1,0:T(8,128)S(1)}, u32[]{:S(2)}, u32[]{:S(2)}) collective-permute-start(f32[20,1104]{1,0:T(8,128)S(1)} %get-tuple-element.9), channel_id=1, source_target_pairs={{8,0},{16,8},{24,16},{32,24},{40,32},{48,40},{56,48},{64,56},{72,6... | collective-permute-start | bytes 264968 | tf_op jit(solution)/shard_map/ppermute | solution.py:20
where the time goes:
time: 359 us; the launch traced here: 358 us
  blocking collectives  240 us (67%)
  other arithmetic  63.7 us (18%)
  starting transfers between devices  21.1 us (6%)
  matrix products  14.2 us (4%)
  waiting for transfers between devices  13.3 us (4%)
  local copies, waits for them, and re-layouts  5.49 us (2%)
    psum x1, blocking collectives, local(): lax.psum((jnp.sum(normed, axis=0), jnp.sum(live_pairs, axis=0)), 'pos')  136 us
    all_gather x1, blocking collectives, local(): weight_all = lax.all_gather(weight, 'pos', axis=0, tiled=True)  76.8 us
    div x1, other arithmetic, local(): donut_enrich = ratios_here / jnp.maximum(donut_sum / donut_cells, 0.25)  49.6 us
    psum x1, blocking collectives, local(): coverage = lax.psum(jnp.sum(kept_counts, axis=1), 'off')  26.7 us
    dot_general x4, matrix products, band_sum(): jnp.dot(rows_block, table, precision=lax.Precision.HIGHEST, preferred_ele...  14.2 us
    ppermute x2, waiting for transfers between devices, padded(): lax.ppermute(head, axis, [((i + 1) % count, i) for i in range(ends)])  12.2 us
    ppermute x2, starting transfers between devices, padded(): lax.ppermute(tail, axis, [(i, (i + 1) % count) for i in range(ends)])  11.6 us
    div x1, other arithmetic, local(): lower_enrich = ratios_here / jnp.maximum(lower_sum / lower_cells, 0.25)  10.4 us
  transfers between devices with their start and end apart: 4, of which 4 were waited for; matrix products, arithmetic and copies ran while one was open for 0% of the time, Pallas kernels for 0%

commit v1 on v0

v1 whole, which is shorter than its diff:
```python
import functools

import jax
import jax.numpy as jnp
from jax import lax
from jax.experimental import pallas as pl
from jax.experimental.pallas import tpu as pltpu
from jax.sharding import PartitionSpec as P

W = 20
P_SIZE = 8
TOP = 24
LANE = 128
SIDE = 64
STEP = 64
SPAN = STEP + 2 * TOP
MESH = pl.DeviceIdType.MESH


def comm_kernel(
    sizes, counts_ref, mask_ref, normed_ref, factor_ref, cells, cov, own, wts, row_w, tables, part, group,
    load_sem, cov_send, cov_recv, halo_send, halo_recv, wts_send, wts_recv, part_send, part_recv, group_send, group_recv,
):
    n_pos, n_off = sizes
    rows, cols = counts_ref.shape
    width = cols + LANE
    blocks = cols // LANE
    ratio = cols // rows
    inner = part.shape[0]
    outer = group.shape[0]
    pos = lax.axis_index("pos")
    off = lax.axis_index("off")
    total_bins = rows * n_pos
    band = cols * n_off
    row_halves = rows // LANE

    def at_pos(k):
        return lax.rem(pos + (k + n_pos), n_pos)

    def at_off(k):
        return lax.rem(off + (k + n_off), n_off)

    first = ratio * off
    quot = pos // inner
    rank = pos - quot * inner
    off_peers = [(pos, at_off(r)) for r in range(1, n_off)]
    halo_peers = [(at_pos(a), at_off(b)) for a in (-1, 1) for b in (-1, 0, 1)]
    steps = list(range(-1, ratio + 2))
    to_wts = [(lax.rem(pos - first - d + n_pos, n_pos), off) for d in steps]
    from_wts = [(lax.rem(pos + first + d + n_pos, n_pos), off) for d in steps]
    part_peers = [(quot * inner + lax.rem(rank + r, inner), off) for r in range(1, inner)]
    group_peers = [(lax.rem(quot + r, outer) * inner + rank, off) for r in range(1, outer)]

    barrier = pltpu.get_barrier_semaphore()

    def greet(device):
        pl.semaphore_signal(barrier, inc=1, device_id=device, device_id_type=MESH)

    for device in off_peers + halo_peers + part_peers + group_peers:
        greet(device)
    for d, there, here in zip(steps, to_wts, from_wts):
        if d == 0:

            @pl.when(off > 0)
            def _():
                greet(there)
                greet(here)
        else:
            greet(there)
            greet(here)

    load = pltpu.make_async_copy(counts_ref, cells.at[pl.ds(TOP, rows), pl.ds(0, cols)], load_sem)
    load.start()
    load.wait()

    base = pos * rows + off * cols
    acc = None
    for b in range(blocks):
        row_i = lax.broadcasted_iota(jnp.int32, (rows, LANE), 0)
        col_i = lax.broadcasted_iota(jnp.int32, (rows, LANE), 1)
        piece = cells[TOP : TOP + rows, b * LANE : (b + 1) * LANE]
        piece = jnp.where(row_i + col_i < total_bins - base - b * LANE, piece, 0.0)
        acc = piece if acc is None else acc + piece
    for h in range(row_halves):
        turned = acc[h * LANE : (h + 1) * LANE, :].T
        cov[0, h : h + 1, :] = jnp.sum(turned, axis=0, keepdims=True)

    n_greet = len(off_peers) + len(halo_peers) + len(part_peers) + len(group_peers) + 2 * (len(steps) - 1)
    pl.semaphore_wait(barrier, n_greet + jnp.where(off > 0, 2, 0))

    def remote(src, dst, send, recv, device):
        return pltpu.make_async_remote_copy(
            src_ref=src, dst_ref=dst, send_sem=send, recv_sem=recv, device_id=device, device_id_type=MESH
        )

    cov_copies = [
        remote(cov.at[0], cov.at[r], cov_send.at[r], cov_recv.at[r], off_peers[r - 1]) for r in range(1, n_off)
    ]
    for copy in cov_copies:
        copy.start()

    spans = {-1: (pl.ds(0, TOP), pl.ds(TOP + rows, TOP)), 1: (pl.ds(rows - TOP, TOP), pl.ds(0, TOP)), 0: (pl.ds(0, rows), pl.ds(TOP, rows))}
    strips = {
        -1: (pl.ds(0, LANE), pl.ds(cols, LANE)),
        1: (pl.ds(cols - LANE, LANE), pl.ds(cols + LANE, LANE)),
        0: (pl.ds(0, cols), pl.ds(0, cols)),
    }
    halo_copies = []
    for a, b in ((0, -1), (0, 1), (-1, 0), (1, 0), (-1, -1), (-1, 1), (1, -1), (1, 1)):
        k = len(halo_copies)
        halo_copies.append(
            remote(
                counts_ref.at[spans[a][0], strips[b][0]],
                cells.at[spans[a][1], strips[b][1]],
                halo_send.at[k],
                halo_recv.at[k],
                (at_pos(a), at_off(b)),
            )
        )
    for copy in halo_copies:
        copy.start()

    for copy in cov_copies:
        copy.wait_recv()
    coverage = cov[0]
    for r in range(1, n_off):
        coverage = coverage + cov[r]
    own[...] = mask_ref[...].astype(jnp.float32) / jnp.sqrt(coverage)

    n_steps = len(steps)
    wts_copies = [
        remote(own, wts.at[k], wts_send.at[k], wts_recv.at[k], to_wts[k]) for k in range(n_steps)
    ]
    for side, a in ((0, 1), (1, -1)):
        k = n_steps + side
        wts_copies.append(remote(own, wts.at[k], wts_send.at[k], wts_recv.at[k], (at_pos(a), off)))
    self_step = steps.index(0)
    for k, copy in enumerate(wts_copies):
        if k == self_step:
            pl.when(off > 0)(copy.start)
        else:
            copy.start()

    @pl.when(off == 0)
    def _():
        wts[self_step] = own[...]

    def down(vector):
        return jnp.broadcast_to(vector, (LANE, LANE)).T

    for h in range(row_halves):
        row_w[TOP + h * LANE : TOP + (h + 1) * LANE, :] = down(own[h : h + 1, :])

    for k, copy in enumerate(wts_copies):
        if k == self_step:
            pl.when(off > 0)(copy.wait_recv)
        else:
            copy.wait_recv()

    pieces = []
    for k, d in enumerate(steps):
        block = pos + first + d
        inside = (block >= 0) & (block < n_pos)
        for h in range(row_halves):
            pieces.append(jnp.where(inside, wts[k, h : h + 1, :], 0.0))
    line = jnp.concatenate(pieces, axis=1)
    reach = line.shape[1]
    line = jnp.broadcast_to(line, (8, reach))
    line = pltpu.roll(line, reach - 7, 1, stride=1, stride_axis=0)
    flip = 7 - lax.broadcasted_iota(jnp.int32, (8, reach), 0)
    line = jnp.take_along_axis(line, flip, axis=0)
    phases = LANE // 8
    for h in range(phases):
        tables[h] = line if h == 0 else pltpu.roll(line, reach - 8 * h, 1)

    low_lanes = lax.broadcasted_iota(jnp.int32, (8, LANE), 1) < SIDE

    def row_group(g):
        rows_g = slice(8 * g, 8 * g + 8)
        place = 8 * g + rows - TOP
        h, shift = (place % LANE) // 8, place // LANE * LANE
        weight = row_w[rows_g, :]
        outs = []
        for b in range(blocks + 1):
            if b < blocks:
                count = cells[rows_g, b * LANE : (b + 1) * LANE]
                col = tables[h, :, shift + b * LANE : shift + (b + 1) * LANE]
            else:
                count = jnp.where(
                    low_lanes, cells[rows_g, cols : cols + LANE], cells[rows_g, cols + LANE : cols + 2 * LANE]
                )
                col = jnp.where(
                    low_lanes,
                    tables[h, :, shift + cols : shift + cols + LANE],
                    tables[h, :, shift - LANE : shift],
                )
            value = count * weight * col
            normed_ref[rows_g, b * LANE : (b + 1) * LANE] = value
            outs.append((value, jnp.where((weight > 0) & (col > 0), 1.0, 0.0)))
        return outs

    halo_copies[0].wait_recv()
    halo_copies[1].wait_recv()
    sums = [None] * (2 * (blocks + 1))
    for g in range(TOP // 8, (TOP + rows) // 8):
        for b, (value, live) in enumerate(row_group(g)):
            for k, term in ((b, value), (blocks + 1 + b, live)):
                sums[k] = term if sums[k] is None else sums[k] + term
    for k, total in enumerate(sums):
        part[0, k : k + 1, :] = jnp.sum(total, axis=0, keepdims=True)

    part_copies = [
        remote(part.at[0], part.at[r], part_send.at[r], part_recv.at[r], part_peers[r - 1]) for r in range(1, inner)
    ]
    for copy in part_copies:
        copy.start()

    for copy in halo_copies[2:]:
        copy.wait_recv()
    for side, h, low, place in ((0, row_halves - 1, LANE - TOP, 0), (1, 0, 0, TOP + rows)):
        block = pos + (1 if side else -1)
        inside = (block >= 0) & (block < n_pos)
        weight = jnp.where(inside, wts[n_steps + side, h : h + 1, :], 0.0)
        row_w[place : place + TOP, :] = down(weight)[low : low + TOP, :]
    for g in list(range(TOP // 8)) + list(range((TOP + rows) // 8, (2 * TOP + rows) // 8)):
        row_group(g)

    for copy in part_copies:
        copy.wait_recv()
    total = part[0]
    for r in range(1, inner):
        total = total + part[r]
    group[0] = total
    group_copies = [
        remote(group.at[0], group.at[r], group_send.at[r], group_recv.at[r], group_peers[r - 1])
        for r in range(1, outer)
    ]
    for copy in group_copies:
        copy.start()
    for copy in group_copies:
        copy.wait_recv()
    total = group[0]
    for r in range(1, outer):
        total = total + group[r]
    expected = total[: blocks + 1, :]
    pairs = total[blocks + 1 :, :]
    lane = lax.broadcasted_iota(jnp.int32, expected.shape, 1)
    place = lax.broadcasted_iota(jnp.int32, expected.shape, 0) * LANE + lane
    place = off * cols + jnp.where(place < cols + SIDE, place, place - width)
    factor = pairs / jnp.where(expected > 0, expected, 1.0)
    factor_ref[...] = jnp.where((place >= 0) & (place < band), factor, 0.0)

    for copy in cov_copies + halo_copies + part_copies + group_copies:
        copy.wait_send()
    for k, copy in enumerate(wts_copies):
        if k == self_step:
            pl.when(off > 0)(copy.wait_send)
        else:
            copy.wait_send()


def near(distance, lowest, highest):
    return (distance >= lowest) & (distance <= highest)


def both(mask_a, mask_b):
    return jnp.where(mask_a | mask_b, 1.0, 0.0).astype(jnp.bfloat16)


def halves(values):
    high = values.astype(jnp.bfloat16)
    return high, (values - high.astype(jnp.float32)).astype(jnp.bfloat16)


def window_kernel(normed_ref, factor_ref, donut_ref, lower_ref, down_table, side_table):
    step = pl.program_id(0)
    width = normed_ref.shape[1]
    cols = donut_ref.shape[1]
    blocks = width // LANE

    @pl.when(step == 0)
    def _():
        out_row = lax.broadcasted_iota(jnp.int32, (STEP, 2 * SPAN), 0)
        out_row = (out_row // 8) * 8 + 7 - lax.rem(out_row, 8)
        in_row = lax.broadcasted_iota(jnp.int32, (STEP, 2 * SPAN), 1)
        in_row = jnp.where(in_row < SPAN, in_row, in_row - SPAN)
        a = in_row - TOP - out_row
        down_table[0:STEP, :] = both(near(a, P_SIZE + 1, W), near(a, -W, -P_SIZE - 1))
        down_table[STEP : 2 * STEP, :] = both(near(a, 1, P_SIZE), near(a, -P_SIZE, -1))
        down_table[2 * STEP : 3 * STEP, :] = both(near(a, P_SIZE + 1, W), near(a, P_SIZE + 1, W))
        down_table[3 * STEP :, :] = both(near(a, 1, P_SIZE), near(a, 1, P_SIZE))
        shape = (2 * LANE, LANE)
        b = lax.broadcasted_iota(jnp.int32, shape, 0) - SIDE - lax.broadcasted_iota(jnp.int32, shape, 1)
        side_table[0] = both(near(b, 1, W), near(b, -W, -1))
        side_table[1] = both(near(b, P_SIZE + 1, W), near(b, -W, -P_SIZE - 1))
        side_table[2] = both(near(b, -W, -1), near(b, -W, -1))
        side_table[3] = both(near(b, -W, -P_SIZE - 1), near(b, -W, -P_SIZE - 1))

    start = pl.multiple_of(step * STEP, STEP)
    factor = jnp.concatenate([factor_ref[b : b + 1, :] for b in range(blocks)], axis=1)
    ratios = normed_ref[pl.ds(start, SPAN), :] * factor
    level = pltpu.roll(ratios, SIDE, 1, stride=1, stride_axis=0)
    stacked = jnp.concatenate(halves(level), axis=0)
    summed = jnp.dot(down_table[...], stacked, preferred_element_type=jnp.float32)

    def sideways(k):
        parts = []
        for half in halves(summed[k * STEP : (k + 1) * STEP, :]):
            around = jnp.concatenate([half, half[:, :LANE]], axis=1)
            parts.append(jnp.concatenate([around[:, b * LANE : (b + 2) * LANE] for b in range(blocks)], axis=0))
        table = side_table[k]
        result = jnp.dot(parts[0], table, preferred_element_type=jnp.float32)
        return result + jnp.dot(parts[1], table, preferred_element_type=jnp.float32)

    flip = 7 - lax.broadcasted_iota(jnp.int32, (8, cols), 0)
    here = ratios[TOP : TOP + STEP, :cols]
    cells_donut = (2 * W + 1) ** 2 - (2 * P_SIZE + 1) ** 2 - 4 * (W - P_SIZE)
    cells_lower = W * W - P_SIZE * P_SIZE
    for out_ref, k, cell_count in ((donut_ref, 0, cells_donut), (lower_ref, 2, cells_lower)):
        tall = sideways(k) + sideways(k + 1)
        flat = jnp.concatenate([tall[b * STEP : (b + 1) * STEP, :] for b in range(blocks)], axis=1)
        for g in range(STEP // 8):
            rows_g = slice(8 * g, 8 * g + 8)
            back = pltpu.roll(flat[rows_g, :], width - TOP - 8 * g - 7, 1, stride=1, stride_axis=0)[:, :cols]
            back = jnp.take_along_axis(back, flip, axis=0)
            out_ref[rows_g, :] = here[rows_g, :] / jnp.maximum(back / cell_count, 0.25)


def local(counts, bin_mask):
    rows, cols = counts.shape
    n_pos = lax.axis_size("pos")
    n_off = lax.axis_size("off")
    inner = 8
    outer = n_pos // inner
    width = cols + LANE
    vecs = 2 * (cols // LANE + 1)
    n_wts = cols // rows + 5
    reach = (cols // rows + 3) * rows
    dma = pltpu.SemaphoreType.DMA
    normed, factor = pl.pallas_call(
        functools.partial(comm_kernel, (n_pos, n_off)),
        out_shape=(
            pltpu.VMEM((rows + 2 * TOP, width), jnp.float32),
            pltpu.VMEM((vecs // 2, LANE), jnp.float32),
        ),
        in_specs=[pl.BlockSpec(memory_space=pl.ANY), pl.BlockSpec(memory_space=pltpu.VMEM)],
        out_specs=(pl.BlockSpec(memory_space=pltpu.VMEM), pl.BlockSpec(memory_space=pltpu.VMEM)),
        scratch_shapes=[
            pltpu.VMEM((rows + 2 * TOP, cols + 2 * LANE), jnp.float32),
            pltpu.VMEM((n_off, rows // LANE, LANE), jnp.float32),
            pltpu.VMEM((rows // LANE, LANE), jnp.float32),
            pltpu.VMEM((n_wts, rows // LANE, LANE), jnp.float32),
            pltpu.VMEM((rows + 2 * TOP, LANE), jnp.float32),
            pltpu.VMEM((LANE // 8, 8, reach), jnp.float32),
            pltpu.VMEM((inner, vecs, LANE), jnp.float32),
            pltpu.VMEM((outer, vecs, LANE), jnp.float32),
            dma,
            dma((n_off,)),
            dma((n_off,)),
            dma((8,)),
            dma((8,)),
            dma((n_wts,)),
            dma((n_wts,)),
            dma((inner,)),
            dma((inner,)),
            dma((outer,)),
            dma((outer,)),
        ],
        compiler_params=pltpu.CompilerParams(
            collective_id=0, has_side_effects=True, vmem_limit_bytes=24 * 1024 * 1024
        ),
        name="comm",
    )(counts, bin_mask.reshape(rows // LANE, LANE))
    out = jax.ShapeDtypeStruct((rows, cols), jnp.float32)
    return pl.pallas_call(
        window_kernel,
        grid=(rows // STEP,),
        out_shape=(out, out),
        in_specs=[pl.BlockSpec(memory_space=pltpu.VMEM), pl.BlockSpec(memory_space=pltpu.VMEM)],
        out_specs=(pl.BlockSpec((STEP, cols), lambda i: (i, 0)), pl.BlockSpec((STEP, cols), lambda i: (i, 0))),
        scratch_shapes=[
            pltpu.VMEM((4 * STEP, 2 * SPAN), jnp.bfloat16),
            pltpu.VMEM((4, 2 * LANE, LANE), jnp.bfloat16),
        ],
        compiler_params=pltpu.CompilerParams(vmem_limit_bytes=24 * 1024 * 1024),
        name="windows",
    )(normed, factor)


def solution(mesh):
    placed = (P("pos", "off"), P("pos"))
    return jax.shard_map(
        local,
        mesh=mesh,
        in_specs=placed,
        out_specs=(P("pos", "off"), P("pos", "off")),
        check_vma=False,
    )
```

time: 359 us -> 45.9 us (0.13)
  the two profiles are of different devices: /device:TPU:38 before, /device:TPU:1 now
where the time goes in v1:
time: 45.9 us; the launch traced here: 45.7 us
  Pallas kernels  43.2 us (94%)
  local copies, waits for them, and re-layouts  1.9 us (4%)
  between operations  0.65 us (1%)
    pallas_call x1, Pallas kernels, local(): pl.pallas_call(functools.partial(comm_kernel, (n_pos, n_off)), out_shape=...  37.6 us
    pallas_call x1, Pallas kernels, local(): pl.pallas_call(window_kernel, grid=(rows // STEP,), out_shape=(out, out),...  5.64 us
    unnamed x4, local copies, waits for them, and re-layouts  1.9 us

profile of v1, /device:TPU:1, one launch (start us, length us, event | category | flops | bytes accessed | tf_op | source)
XLA Modules:
  0.0 45.7 jit_solution(3700311638993572758)
XLA Ops:
  0.6 0.0 copy-start
  0.6 1.2 %copy-done = f32[256,1024]{1,0:T(8,128)S(1)} copy-done((f32[256,1024]{1,0:T(8,128)S(1)}, f32[256,1024]{1,0:T(8,128)}, u32[]{:S(2)}) %copy-start) | copy-done | bytes 1048600
  1.9 0.0 copy-start.1
  1.9 0.7 %copy-done.1 = s32[256]{0:T(256)S(1)} copy-done((s32[256]{0:T(256)S(1)}, s32[256]{0:T(256)}, u32[]{:S(2)}) %copy-start.1) | copy-done | bytes 1048
  2.5 37.6 %comm.1 = (f32[304,1152]{1,0:T(8,128)S(1)}, f32[9,128]{1,0:T(8,128)S(1)}) custom-call(f32[256,1024]{1,0:T(8,128)S(1)} %copy-done, s32[2,128]{1,0:T(2,128)S(1)} %bitcast.1), custom_call_target="tpu_custom_call" | custom-call | tf_op jit(solution)/shard_map/comm/pallas_call | solution.py:340
  40.1 5.6 %windows.1 = (f32[256,1024]{1,0:T(8,128)}, f32[256,1024]{1,0:T(8,128)}) custom-call(f32[304,1152]{1,0:T(8,128)S(1)} %get-tuple-element.4.normed_ref, f32[9,128]{1,0:T(8,128)S(1)} %get-tuple-element.5.factor_ref), custom_call_target="tpu_custom_call" | custom-call | tf_op jit(solution)/shard_map/windows/pallas_call | solution.py:375
Async XLA Ops:
  0.6 1.2 %copy-start = (f32[256,1024]{1,0:T(8,128)S(1)}, f32[256,1024]{1,0:T(8,128)}, u32[]{:S(2)}) copy-start(f32[256,1024]{1,0:T(8,128)} %counts_ref.1) | copy-start | bytes 3145732
  1.9 0.7 %copy-start.1 = (s32[256]{0:T(256)S(1)}, s32[256]{0:T(256)}, u32[]{:S(2)}) copy-start(s32[256]{0:T(256)} %param.3) | copy-start | bytes 3076

commit v2 on v1

--- a/solution.py
+++ b/solution.py
@@ -18,14 +18,17 @@
 
 
 def comm_kernel(
-    sizes, counts_ref, mask_ref, normed_ref, factor_ref, cells, cov, own, wts, row_w, tables, part, group,
-    load_sem, cov_send, cov_recv, halo_send, halo_recv, wts_send, wts_recv, part_send, part_recv, group_send, group_recv,
+    sizes, counts_ref, mask_ref, normed_ref, factor_ref,
+    cells, strips_out, strips_in, mask, cov, own, wts, lines, row_w, tables, part, group,
+    load_sem, mask_sem, cov_send, cov_recv, halo_send, halo_recv, wts_send, wts_recv, part_send, part_recv, group_send, group_recv,
 ):
     n_pos, n_off = sizes
     rows, cols = counts_ref.shape
     width = cols + LANE
     blocks = cols // LANE
     ratio = cols // rows
+    near_offs = cov.shape[0]
+    far_offs = n_off // near_offs
     inner = part.shape[0]
     outer = group.shape[0]
     pos = lax.axis_index("pos")
@@ -33,6 +36,7 @@
     total_bins = rows * n_pos
     band = cols * n_off
     row_halves = rows // LANE
+    third = strips_in.shape[1]
 
     def at_pos(k):
         return lax.rem(pos + (k + n_pos), n_pos)
@@ -41,36 +45,71 @@
         return lax.rem(off + (k + n_off), n_off)
 
     first = ratio * off
+    far = off // near_offs
+    near = off - far * near_offs
     quot = pos // inner
     rank = pos - quot * inner
-    off_peers = [(pos, at_off(r)) for r in range(1, n_off)]
-    halo_peers = [(at_pos(a), at_off(b)) for a in (-1, 1) for b in (-1, 0, 1)]
+    cov_peers = [(pos, far * near_offs + lax.rem(near + r, near_offs)) for r in range(1, near_offs)]
+    halo_moves = [(0, -1), (0, 1), (-1, 0), (1, 0), (-1, -1), (-1, 1), (1, -1), (1, 1)]
     steps = list(range(-1, ratio + 2))
-    to_wts = [(lax.rem(pos - first - d + n_pos, n_pos), off) for d in steps]
-    from_wts = [(lax.rem(pos + first + d + n_pos, n_pos), off) for d in steps]
+    n_steps = len(steps)
+    self_step = steps.index(0)
+    n_slots = n_steps + 3
     part_peers = [(quot * inner + lax.rem(rank + r, inner), off) for r in range(1, inner)]
     group_peers = [(lax.rem(quot + r, outer) * inner + rank, off) for r in range(1, outer)]
 
+    def wts_target(t, slot):
+        there = lax.rem(far + t, far_offs) * near_offs + near
+        if slot < n_steps:
+            return (lax.rem(pos - ratio * there - steps[slot] + n_pos, n_pos), there)
+        return (at_pos((1, -1, 0)[slot - n_steps]), there)
+
+    def wts_source(t, slot):
+        there = lax.rem(far - t + far_offs, far_offs) * near_offs + near
+        if slot < n_steps:
+            return (lax.rem(pos + first + steps[slot] + n_pos, n_pos), there)
+        return (at_pos((-1, 1, 0)[slot - n_steps]), there)
+
+    moves = []
+    for t in list(range(1, far_offs)) + [0]:
+        for slot in range(n_slots):
+            if t or slot != n_slots - 1:
+                moves.append((t, slot, t == 0 and slot == self_step))
+
     barrier = pltpu.get_barrier_semaphore()
 
     def greet(device):
         pl.semaphore_signal(barrier, inc=1, device_id=device, device_id_type=MESH)
 
-    for device in off_peers + halo_peers + part_peers + group_peers:
+    for device in cov_peers:
         greet(device)
-    for d, there, here in zip(steps, to_wts, from_wts):
-        if d == 0:
-
-            @pl.when(off > 0)
-            def _():
-                greet(there)
-                greet(here)
+    for t, slot, selfish in moves:
+        if selfish:
+            pl.when(off > 0)(functools.partial(greet, wts_source(t, slot)))
         else:
-            greet(there)
-            greet(here)
+            greet(wts_source(t, slot))
+    for a, b in halo_moves:
+        greet((at_pos(-a), at_off(-b)))
+    for device in part_peers + group_peers:
+        greet(device)
 
     load = pltpu.make_async_copy(counts_ref, cells.at[pl.ds(TOP, rows), pl.ds(0, cols)], load_sem)
     load.start()
+    load_mask = pltpu.make_async_copy(mask_ref, mask, mask_sem)
+    load_mask.start()
+
+    @pl.when(off == 0)
+    def _():
+        strips_in[1] = jnp.zeros(strips_in.shape[1:], jnp.float32)
+        for place in (0, TOP + rows):
+            cells[place : place + TOP, cols + LANE :] = jnp.zeros((TOP, LANE), jnp.float32)
+
+    @pl.when(off == n_off - 1)
+    def _():
+        strips_in[0] = jnp.zeros(strips_in.shape[1:], jnp.float32)
+        for place in (0, TOP + rows):
+            cells[place : place + TOP, cols : cols + LANE] = jnp.zeros((TOP, LANE), jnp.float32)
+
     load.wait()
 
     base = pos * rows + off * cols
@@ -84,9 +123,10 @@
     for h in range(row_halves):
         turned = acc[h * LANE : (h + 1) * LANE, :].T
         cov[0, h : h + 1, :] = jnp.sum(turned, axis=0, keepdims=True)
-
-    n_greet = len(off_peers) + len(halo_peers) + len(part_peers) + len(group_peers) + 2 * (len(steps) - 1)
-    pl.semaphore_wait(barrier, n_greet + jnp.where(off > 0, 2, 0))
+    load_mask.wait()
+
+    n_greet = len(cov_peers) + len(moves) - 1 + len(halo_moves) + len(part_peers) + len(group_peers)
+    pl.semaphore_wait(barrier, n_greet + jnp.where(off > 0, 1, 0))
 
     def remote(src, dst, send, recv, device):
         return pltpu.make_async_remote_copy(
@@ -94,75 +134,106 @@
         )
 
     cov_copies = [
-        remote(cov.at[0], cov.at[r], cov_send.at[r], cov_recv.at[r], off_peers[r - 1]) for r in range(1, n_off)
+        remote(cov.at[0], cov.at[r], cov_send.at[r], cov_recv.at[r], cov_peers[r - 1]) for r in range(1, near_offs)
     ]
     for copy in cov_copies:
         copy.start()
 
-    spans = {-1: (pl.ds(0, TOP), pl.ds(TOP + rows, TOP)), 1: (pl.ds(rows - TOP, TOP), pl.ds(0, TOP)), 0: (pl.ds(0, rows), pl.ds(TOP, rows))}
+    spare = LANE // 3
+    lane_t = lax.broadcasted_iota(jnp.int32, (third, LANE), 1)
+    for side in (0, 1):
+        packed = None
+        for k in range(3):
+            low = TOP + k * third
+            high = min(low + third, TOP + rows)
+            piece = cells[low:high, 0:LANE] if side == 0 else cells[low:high, cols - LANE : cols]
+            if high - low < third:
+                piece = jnp.concatenate([piece, jnp.zeros((third - high + low, LANE), jnp.float32)], axis=0)
+            if side == 0:
+                piece = pltpu.roll(piece, k * spare, 1) if k else piece
+                here = (lane_t >= k * spare) & (lane_t < (k + 1) * spare)
+            else:
+                piece = pltpu.roll(piece, LANE - k * spare, 1) if k else piece
+                here = (lane_t < LANE - k * spare) & (lane_t >= LANE - (k + 1) * spare)
+            packed = jnp.where(here, piece, 0.0 if packed is None else packed)
+        strips_out[side] = packed
+
+    spans = {-1: (pl.ds(0, TOP), pl.ds(TOP + rows, TOP)), 1: (pl.ds(rows - TOP, TOP), pl.ds(0, TOP))}
     strips = {
         -1: (pl.ds(0, LANE), pl.ds(cols, LANE)),
         1: (pl.ds(cols - LANE, LANE), pl.ds(cols + LANE, LANE)),
         0: (pl.ds(0, cols), pl.ds(0, cols)),
     }
     halo_copies = []
-    for a, b in ((0, -1), (0, 1), (-1, 0), (1, 0), (-1, -1), (-1, 1), (1, -1), (1, 1)):
-        k = len(halo_copies)
-        halo_copies.append(
-            remote(
-                counts_ref.at[spans[a][0], strips[b][0]],
-                cells.at[spans[a][1], strips[b][1]],
-                halo_send.at[k],
-                halo_recv.at[k],
-                (at_pos(a), at_off(b)),
-            )
-        )
-    for copy in halo_copies:
-        copy.start()
+    for k, (a, b) in enumerate(halo_moves):
+        if a == 0:
+            side = 0 if b < 0 else 1
+            ends = strips_out.at[side], strips_in.at[side]
+        else:
+            ends = counts_ref.at[spans[a][0], strips[b][0]], cells.at[spans[a][1], strips[b][1]]
+        halo_copies.append(remote(*ends, halo_send.at[k], halo_recv.at[k], (at_pos(a), at_off(b))))
+
+    def sends(b):
+        return off > 0 if b < 0 else off < n_off - 1
+
+    def each_halo(copies, act):
+        for (a, b), copy in copies:
+            if b == 0:
+                getattr(copy, act)()
+            elif act == "wait_recv":
+                pl.when(sends(-b))(copy.wait_recv)
+            else:
+                pl.when(sends(b))(getattr(copy, act))
+
+    halos = list(zip(halo_moves, halo_copies))
+    each_halo(halos, "start")
 
     for copy in cov_copies:
         copy.wait_recv()
     coverage = cov[0]
-    for r in range(1, n_off):
+    for r in range(1, near_offs):
         coverage = coverage + cov[r]
-    own[...] = mask_ref[...].astype(jnp.float32) / jnp.sqrt(coverage)
-
-    n_steps = len(steps)
+    own[0:row_halves, :] = coverage
+    own[row_halves:, :] = mask[...].astype(jnp.float32)
+
     wts_copies = [
-        remote(own, wts.at[k], wts_send.at[k], wts_recv.at[k], to_wts[k]) for k in range(n_steps)
+        remote(own, wts.at[t, slot], wts_send.at[t, slot], wts_recv.at[t, slot], wts_target(t, slot))
+        for t, slot, _ in moves
     ]
-    for side, a in ((0, 1), (1, -1)):
-        k = n_steps + side
-        wts_copies.append(remote(own, wts.at[k], wts_send.at[k], wts_recv.at[k], (at_pos(a), off)))
-    self_step = steps.index(0)
-    for k, copy in enumerate(wts_copies):
-        if k == self_step:
-            pl.when(off > 0)(copy.start)
-        else:
-            copy.start()
+
+    def each_wts(act):
+        for (_, _, selfish), copy in zip(moves, wts_copies):
+            if selfish:
+                pl.when(off > 0)(getattr(copy, act))
+            else:
+                getattr(copy, act)()
+
+    each_wts("start")
+    wts[0, n_slots - 1] = own[...]
 
     @pl.when(off == 0)
     def _():
-        wts[self_step] = own[...]
+        wts[0, self_step] = own[...]
+
+    each_wts("wait_recv")
+
+    gathered = wts[0, :, 0:row_halves, :]
+    for t in range(1, far_offs):
+        gathered = gathered + wts[t, :, 0:row_halves, :]
+    lines[...] = wts[0, :, row_halves:, :] / jnp.sqrt(gathered)
 
     def down(vector):
         return jnp.broadcast_to(vector, (LANE, LANE)).T
 
     for h in range(row_halves):
-        row_w[TOP + h * LANE : TOP + (h + 1) * LANE, :] = down(own[h : h + 1, :])
-
-    for k, copy in enumerate(wts_copies):
-        if k == self_step:
-            pl.when(off > 0)(copy.wait_recv)
-        else:
-            copy.wait_recv()
+        row_w[TOP + h * LANE : TOP + (h + 1) * LANE, :] = down(lines[n_slots - 1, h : h + 1, :])
 
     pieces = []
     for k, d in enumerate(steps):
         block = pos + first + d
         inside = (block >= 0) & (block < n_pos)
         for h in range(row_halves):
-            pieces.append(jnp.where(inside, wts[k, h : h + 1, :], 0.0))
+            pieces.append(jnp.where(inside, lines[k, h : h + 1, :], 0.0))
     line = jnp.concatenate(pieces, axis=1)
     reach = line.shape[1]
     line = jnp.broadcast_to(line, (8, reach))
@@ -173,7 +244,8 @@
     for h in range(phases):
         tables[h] = line if h == 0 else pltpu.roll(line, reach - 8 * h, 1)
 
-    low_lanes = lax.broadcasted_iota(jnp.int32, (8, LANE), 1) < SIDE
+    lane_8 = lax.broadcasted_iota(jnp.int32, (8, LANE), 1)
+    low_lanes = lane_8 < SIDE
 
     def row_group(g):
         rows_g = slice(8 * g, 8 * g + 8)
@@ -186,9 +258,16 @@
                 count = cells[rows_g, b * LANE : (b + 1) * LANE]
                 col = tables[h, :, shift + b * LANE : shift + (b + 1) * LANE]
             else:
-                count = jnp.where(
-                    low_lanes, cells[rows_g, cols : cols + LANE], cells[rows_g, cols + LANE : cols + 2 * LANE]
-                )
+                own_row = 8 * g - TOP
+                if 0 <= own_row < rows:
+                    k, at = own_row // third, own_row % third
+                    after, before = strips_in[0, at : at + 8, :], strips_in[1, at : at + 8, :]
+                    if k:
+                        after = pltpu.roll(after, LANE - k * spare, 1)
+                        before = pltpu.roll(before, k * spare, 1)
+                else:
+                    after, before = cells[rows_g, cols : cols + LANE], cells[rows_g, cols + LANE : cols + 2 * LANE]
+                count = jnp.where(low_lanes, after, before)
                 col = jnp.where(
                     low_lanes,
                     tables[h, :, shift + cols : shift + cols + LANE],
@@ -199,8 +278,7 @@
             outs.append((value, jnp.where((weight > 0) & (col > 0), 1.0, 0.0)))
         return outs
 
-    halo_copies[0].wait_recv()
-    halo_copies[1].wait_recv()
+    each_halo(halos[:2], "wait_recv")
     sums = [None] * (2 * (blocks + 1))
     for g in range(TOP // 8, (TOP + rows) // 8):
         for b, (value, live) in enumerate(row_group(g)):
@@ -215,12 +293,11 @@
     for copy in part_copies:
         copy.start()
 
-    for copy in halo_copies[2:]:
-        copy.wait_recv()
+    each_halo(halos[2:], "wait_recv")
     for side, h, low, place in ((0, row_halves - 1, LANE - TOP, 0), (1, 0, 0, TOP + rows)):
         block = pos + (1 if side else -1)
         inside = (block >= 0) & (block < n_pos)
-        weight = jnp.where(inside, wts[n_steps + side, h : h + 1, :], 0.0)
+        weight = jnp.where(inside, lines[n_steps + side, h : h + 1, :], 0.0)
         row_w[place : place + TOP, :] = down(weight)[low : low + TOP, :]
     for g in list(range(TOP // 8)) + list(range((TOP + rows) // 8, (2 * TOP + rows) // 8)):
         row_group(g)
@@ -237,6 +314,10 @@
     ]
     for copy in group_copies:
         copy.start()
+    for copy in cov_copies + part_copies:
+        copy.wait_send()
+    each_halo(halos, "wait_send")
+    each_wts("wait_send")
     for copy in group_copies:
         copy.wait_recv()
     total = group[0]
@@ -246,17 +327,12 @@
     pairs = total[blocks + 1 :, :]
     lane = lax.broadcasted_iota(jnp.int32, expected.shape, 1)
     place = lax.broadcasted_iota(jnp.int32, expected.shape, 0) * LANE + lane
+    needed = (place < cols + 2 * W) | (place >= width - 2 * W)
     place = off * cols + jnp.where(place < cols + SIDE, place, place - width)
     factor = pairs / jnp.where(expected > 0, expected, 1.0)
-    factor_ref[...] = jnp.where((place >= 0) & (place < band), factor, 0.0)
-
-    for copy in cov_copies + halo_copies + part_copies + group_copies:
+    factor_ref[...] = jnp.where(needed & (place >= 0) & (place < band), factor, 0.0)
+    for copy in group_copies:
         copy.wait_send()
-    for k, copy in enumerate(wts_copies):
-        if k == self_step:
-            pl.when(off > 0)(copy.wait_send)
-        else:
-            copy.wait_send()
 
 
 def near(distance, lowest, highest):
@@ -332,35 +408,45 @@
     n_off = lax.axis_size("off")
     inner = 8
     outer = n_pos // inner
+    near_offs = 4
+    far_offs = n_off // near_offs
     width = cols + LANE
     vecs = 2 * (cols // LANE + 1)
-    n_wts = cols // rows + 5
+    n_slots = cols // rows + 6
     reach = (cols // rows + 3) * rows
+    halves_n = rows // LANE
+    third = -(-rows // 24) * 8
     dma = pltpu.SemaphoreType.DMA
+    f32 = jnp.float32
     normed, factor = pl.pallas_call(
         functools.partial(comm_kernel, (n_pos, n_off)),
         out_shape=(
-            pltpu.VMEM((rows + 2 * TOP, width), jnp.float32),
-            pltpu.VMEM((vecs // 2, LANE), jnp.float32),
+            pltpu.VMEM((rows + 2 * TOP, width), f32),
+            pltpu.VMEM((vecs // 2, LANE), f32),
         ),
-        in_specs=[pl.BlockSpec(memory_space=pl.ANY), pl.BlockSpec(memory_space=pltpu.VMEM)],
+        in_specs=[pl.BlockSpec(memory_space=pltpu.HBM), pl.BlockSpec(memory_space=pltpu.HBM)],
         out_specs=(pl.BlockSpec(memory_space=pltpu.VMEM), pl.BlockSpec(memory_space=pltpu.VMEM)),
         scratch_shapes=[
-            pltpu.VMEM((rows + 2 * TOP, cols + 2 * LANE), jnp.float32),
-            pltpu.VMEM((n_off, rows // LANE, LANE), jnp.float32),
-            pltpu.VMEM((rows // LANE, LANE), jnp.float32),
-            pltpu.VMEM((n_wts, rows // LANE, LANE), jnp.float32),
-            pltpu.VMEM((rows + 2 * TOP, LANE), jnp.float32),
-            pltpu.VMEM((LANE // 8, 8, reach), jnp.float32),
-            pltpu.VMEM((inner, vecs, LANE), jnp.float32),
-            pltpu.VMEM((outer, vecs, LANE), jnp.float32),
+            pltpu.VMEM((rows + 2 * TOP, cols + 2 * LANE), f32),
+            pltpu.VMEM((2, third, LANE), f32),
+            pltpu.VMEM((2, third, LANE), f32),
+            pltpu.VMEM((halves_n, LANE), jnp.int32),
+            pltpu.VMEM((near_offs, halves_n, LANE), f32),
+            pltpu.VMEM((2 * halves_n, LANE), f32),
+            pltpu.VMEM((far_offs, n_slots, 2 * halves_n, LANE), f32),
+            pltpu.VMEM((n_slots, halves_n, LANE), f32),
+            pltpu.VMEM((rows + 2 * TOP, LANE), f32),
+            pltpu.VMEM((LANE // 8, 8, reach), f32),
+            pltpu.VMEM((inner, vecs, LANE), f32),
+            pltpu.VMEM((outer, vecs, LANE), f32),
             dma,
-            dma((n_off,)),
-            dma((n_off,)),
+            dma,
+            dma((near_offs,)),
+            dma((near_offs,)),
             dma((8,)),
             dma((8,)),
-            dma((n_wts,)),
-            dma((n_wts,)),
+            dma((far_offs, n_slots)),
+            dma((far_offs, n_slots)),
             dma((inner,)),
             dma((inner,)),
             dma((outer,)),
@@ -370,7 +456,10 @@
             collective_id=0, has_side_effects=True, vmem_limit_bytes=24 * 1024 * 1024
         ),
         name="comm",
-    )(counts, bin_mask.reshape(rows // LANE, LANE))
+    )(
+        pltpu.with_memory_space_constraint(counts, pltpu.HBM),
+        pltpu.with_memory_space_constraint(bin_mask.reshape(halves_n, LANE), pltpu.HBM),
+    )
     out = jax.ShapeDtypeStruct((rows, cols), jnp.float32)
     return pl.pallas_call(
         window_kernel,

time: 45.9 us -> 40.1 us (0.87)
  Pallas kernels: 43.2 us -> 39.3 us
  local copies, waits for them, and re-layouts: 1.9 us -> 0 us
    pallas_call x1, Pallas kernels: 37.6 us -> 33.6 us  [local(): pl.pallas_call(functools.partial(comm_kernel, (n_pos, n_off)), out_shape=...]
    unnamed x4 -> x0, local copies, waits for them, and re-layouts: 1.9 us -> none
where the time goes in v2:
time: 40.1 us; the launch traced here: 39.9 us
  Pallas kernels  39.3 us (98%)
  between operations  0.64 us (2%)
    pallas_call x1, Pallas kernels, local(): pl.pallas_call(functools.partial(comm_kernel, (n_pos, n_off)), out_shape=...  33.6 us
    pallas_call x1, Pallas kernels, local(): pl.pallas_call(window_kernel, grid=(rows // STEP,), out_shape=(out, out),...  5.64 us

profile of v2, /device:TPU:1, one launch (start us, length us, event | category | flops | bytes accessed | tf_op | source)
XLA Modules:
  0.0 39.9 jit_solution(13029043495978563936)
XLA Ops:
  0.6 33.6 %comm.1 = (f32[304,1152]{1,0:T(8,128)S(1)}, f32[9,128]{1,0:T(8,128)S(1)}) custom-call(f32[256,1024]{1,0:T(8,128)} %counts_ref.1, s32[2,128]{1,0:T(2,128)} %bitcast.1), custom_call_target="tpu_custom_call" | custom-call | tf_op jit(solution)/shard_map/comm/pallas_call | solution.py:421
  34.3 5.6 %windows.1 = (f32[256,1024]{1,0:T(8,128)}, f32[256,1024]{1,0:T(8,128)}) custom-call(f32[304,1152]{1,0:T(8,128)S(1)} %get-tuple-element.4.normed_ref, f32[9,128]{1,0:T(8,128)S(1)} %get-tuple-element.5.factor_ref), custom_call_target="tpu_custom_call" | custom-call | tf_op jit(solution)/shard_map/windows/pallas_call | solution.py:464

commit v3 on v2

--- a/solution.py
+++ b/solution.py
@@ -76,6 +76,11 @@
             if t or slot != n_slots - 1:
                 moves.append((t, slot, t == 0 and slot == self_step))
 
+    load = pltpu.make_async_copy(counts_ref, cells.at[pl.ds(TOP, rows), pl.ds(0, cols)], load_sem)
+    load.start()
+    load_mask = pltpu.make_async_copy(mask_ref, mask, mask_sem)
+    load_mask.start()
+
     barrier = pltpu.get_barrier_semaphore()
 
     def greet(device):
@@ -92,11 +97,6 @@
         greet((at_pos(-a), at_off(-b)))
     for device in part_peers + group_peers:
         greet(device)
-
-    load = pltpu.make_async_copy(counts_ref, cells.at[pl.ds(TOP, rows), pl.ds(0, cols)], load_sem)
-    load.start()
-    load_mask = pltpu.make_async_copy(mask_ref, mask, mask_sem)
-    load_mask.start()
 
     @pl.when(off == 0)
     def _():
@@ -186,7 +186,7 @@
                 pl.when(sends(b))(getattr(copy, act))
 
     halos = list(zip(halo_moves, halo_copies))
-    each_halo(halos, "start")
+    each_halo(halos[:2], "start")
 
     for copy in cov_copies:
         copy.wait_recv()
@@ -216,6 +216,7 @@
         wts[0, self_step] = own[...]
 
     each_wts("wait_recv")
+    each_halo(halos[2:], "start")
 
     gathered = wts[0, :, 0:row_halves, :]
     for t in range(1, far_offs):
@@ -293,15 +294,6 @@
     for copy in part_copies:
         copy.start()
 
-    each_halo(halos[2:], "wait_recv")
-    for side, h, low, place in ((0, row_halves - 1, LANE - TOP, 0), (1, 0, 0, TOP + rows)):
-        block = pos + (1 if side else -1)
-        inside = (block >= 0) & (block < n_pos)
-        weight = jnp.where(inside, lines[n_steps + side, h : h + 1, :], 0.0)
-        row_w[place : place + TOP, :] = down(weight)[low : low + TOP, :]
-    for g in list(range(TOP // 8)) + list(range((TOP + rows) // 8, (2 * TOP + rows) // 8)):
-        row_group(g)
-
     for copy in part_copies:
         copy.wait_recv()
     total = part[0]
@@ -314,6 +306,15 @@
     ]
     for copy in group_copies:
         copy.start()
+    each_halo(halos[2:], "wait_recv")
+    for side, h, low, place in ((0, row_halves - 1, LANE - TOP, 0), (1, 0, 0, TOP + rows)):
+        block = pos + (1 if side else -1)
+        inside = (block >= 0) & (block < n_pos)
+        weight = jnp.where(inside, lines[n_steps + side, h : h + 1, :], 0.0)
+        row_w[place : place + TOP, :] = down(weight)[low : low + TOP, :]
+    for g in list(range(TOP // 8)) + list(range((TOP + rows) // 8, (2 * TOP + rows) // 8)):
+        row_group(g)
+
     for copy in cov_copies + part_copies:
         copy.wait_send()
     each_halo(halos, "wait_send")

time: 40.1 us -> 42.1 us (1.050)
  Pallas kernels: 39.3 us -> 41.3 us
    pallas_call x1, Pallas kernels: 33.6 us -> 35.7 us  [local(): pl.pallas_call(functools.partial(comm_kernel, (n_pos, n_off)), out_shape=...]
where the time goes in v3:
time: 42.1 us; the launch traced here: 41.9 us
  Pallas kernels  41.3 us (98%)
  between operations  0.64 us (2%)
    pallas_call x1, Pallas kernels, local(): pl.pallas_call(functools.partial(comm_kernel, (n_pos, n_off)), out_shape=...  35.7 us
    pallas_call x1, Pallas kernels, local(): pl.pallas_call(window_kernel, grid=(rows // STEP,), out_shape=(out, out),...  5.64 us

profile of v3, /device:TPU:1, one launch (start us, length us, event | category | flops | bytes accessed | tf_op | source)
XLA Modules:
  0.0 41.9 jit_solution(18055253834636726255)
XLA Ops:
  0.6 35.7 %comm.1 = (f32[304,1152]{1,0:T(8,128)S(1)}, f32[9,128]{1,0:T(8,128)S(1)}) custom-call(f32[256,1024]{1,0:T(8,128)} %counts_ref.1, s32[2,128]{1,0:T(2,128)} %bitcast.1), custom_call_target="tpu_custom_call" | custom-call | tf_op jit(solution)/shard_map/comm/pallas_call | solution.py:422
  36.3 5.6 %windows.1 = (f32[256,1024]{1,0:T(8,128)}, f32[256,1024]{1,0:T(8,128)}) custom-call(f32[304,1152]{1,0:T(8,128)S(1)} %get-tuple-element.4.normed_ref, f32[9,128]{1,0:T(8,128)S(1)} %get-tuple-element.5.factor_ref), custom_call_target="tpu_custom_call" | custom-call | tf_op jit(solution)/shard_map/windows/pallas_call | solution.py:465

commit v4 on v2

--- a/solution.py
+++ b/solution.py
@@ -76,6 +76,11 @@
             if t or slot != n_slots - 1:
                 moves.append((t, slot, t == 0 and slot == self_step))
 
+    load = pltpu.make_async_copy(counts_ref, cells.at[pl.ds(TOP, rows), pl.ds(0, cols)], load_sem)
+    load.start()
+    load_mask = pltpu.make_async_copy(mask_ref, mask, mask_sem)
+    load_mask.start()
+
     barrier = pltpu.get_barrier_semaphore()
 
     def greet(device):
@@ -92,11 +97,6 @@
         greet((at_pos(-a), at_off(-b)))
     for device in part_peers + group_peers:
         greet(device)
-
-    load = pltpu.make_async_copy(counts_ref, cells.at[pl.ds(TOP, rows), pl.ds(0, cols)], load_sem)
-    load.start()
-    load_mask = pltpu.make_async_copy(mask_ref, mask, mask_sem)
-    load_mask.start()
 
     @pl.when(off == 0)
     def _():
@@ -138,6 +138,36 @@
     ]
     for copy in cov_copies:
         copy.start()
+
+    spans = {-1: (pl.ds(0, TOP), pl.ds(TOP + rows, TOP)), 1: (pl.ds(rows - TOP, TOP), pl.ds(0, TOP))}
+    strips = {
+        -1: (pl.ds(0, LANE), pl.ds(cols, LANE)),
+        1: (pl.ds(cols - LANE, LANE), pl.ds(cols + LANE, LANE)),
+        0: (pl.ds(0, cols), pl.ds(0, cols)),
+    }
+    halo_copies = []
+    for k, (a, b) in enumerate(halo_moves):
+        if a == 0:
+            side = 0 if b < 0 else 1
+            ends = strips_out.at[side], strips_in.at[side]
+        else:
+            ends = counts_ref.at[spans[a][0], strips[b][0]], cells.at[spans[a][1], strips[b][1]]
+        halo_copies.append(remote(*ends, halo_send.at[k], halo_recv.at[k], (at_pos(a), at_off(b))))
+
+    def sends(b):
+        return off > 0 if b < 0 else off < n_off - 1
+
+    def each_halo(copies, act):
+        for (a, b), copy in copies:
+            if b == 0:
+                getattr(copy, act)()
+            elif act == "wait_recv":
+                pl.when(sends(-b))(copy.wait_recv)
+            else:
+                pl.when(sends(b))(getattr(copy, act))
+
+    halos = list(zip(halo_moves, halo_copies))
+    each_halo(halos[2:], "start")
 
     spare = LANE // 3
     lane_t = lax.broadcasted_iota(jnp.int32, (third, LANE), 1)
@@ -158,35 +188,7 @@
             packed = jnp.where(here, piece, 0.0 if packed is None else packed)
         strips_out[side] = packed
 
-    spans = {-1: (pl.ds(0, TOP), pl.ds(TOP + rows, TOP)), 1: (pl.ds(rows - TOP, TOP), pl.ds(0, TOP))}
-    strips = {
-        -1: (pl.ds(0, LANE), pl.ds(cols, LANE)),
-        1: (pl.ds(cols - LANE, LANE), pl.ds(cols + LANE, LANE)),
-        0: (pl.ds(0, cols), pl.ds(0, cols)),
-    }
-    halo_copies = []
-    for k, (a, b) in enumerate(halo_moves):
-        if a == 0:
-            side = 0 if b < 0 else 1
-            ends = strips_out.at[side], strips_in.at[side]
-        else:
-            ends = counts_ref.at[spans[a][0], strips[b][0]], cells.at[spans[a][1], strips[b][1]]
-        halo_copies.append(remote(*ends, halo_send.at[k], halo_recv.at[k], (at_pos(a), at_off(b))))
-
-    def sends(b):
-        return off > 0 if b < 0 else off < n_off - 1
-
-    def each_halo(copies, act):
-        for (a, b), copy in copies:
-            if b == 0:
-                getattr(copy, act)()
-            elif act == "wait_recv":
-                pl.when(sends(-b))(copy.wait_recv)
-            else:
-                pl.when(sends(b))(getattr(copy, act))
-
-    halos = list(zip(halo_moves, halo_copies))
-    each_halo(halos, "start")
+    each_halo(halos[:2], "start")
 
     for copy in cov_copies:
         copy.wait_recv()
@@ -348,58 +350,89 @@
     return high, (values - high.astype(jnp.float32)).astype(jnp.bfloat16)
 
 
-def window_kernel(normed_ref, factor_ref, donut_ref, lower_ref, down_table, side_table):
-    step = pl.program_id(0)
+def window_kernel(normed_ref, factor_ref, donut_ref, lower_ref, donut, lower, sems):
     width = normed_ref.shape[1]
-    cols = donut_ref.shape[1]
+    rows, cols = donut_ref.shape
     blocks = width // LANE
 
-    @pl.when(step == 0)
-    def _():
-        out_row = lax.broadcasted_iota(jnp.int32, (STEP, 2 * SPAN), 0)
-        out_row = (out_row // 8) * 8 + 7 - lax.rem(out_row, 8)
-        in_row = lax.broadcasted_iota(jnp.int32, (STEP, 2 * SPAN), 1)
-        in_row = jnp.where(in_row < SPAN, in_row, in_row - SPAN)
-        a = in_row - TOP - out_row
-        down_table[0:STEP, :] = both(near(a, P_SIZE + 1, W), near(a, -W, -P_SIZE - 1))
-        down_table[STEP : 2 * STEP, :] = both(near(a, 1, P_SIZE), near(a, -P_SIZE, -1))
-        down_table[2 * STEP : 3 * STEP, :] = both(near(a, P_SIZE + 1, W), near(a, P_SIZE + 1, W))
-        down_table[3 * STEP :, :] = both(near(a, 1, P_SIZE), near(a, 1, P_SIZE))
-        shape = (2 * LANE, LANE)
-        b = lax.broadcasted_iota(jnp.int32, shape, 0) - SIDE - lax.broadcasted_iota(jnp.int32, shape, 1)
-        side_table[0] = both(near(b, 1, W), near(b, -W, -1))
-        side_table[1] = both(near(b, P_SIZE + 1, W), near(b, -W, -P_SIZE - 1))
-        side_table[2] = both(near(b, -W, -1), near(b, -W, -1))
-        side_table[3] = both(near(b, -W, -P_SIZE - 1), near(b, -W, -P_SIZE - 1))
-
-    start = pl.multiple_of(step * STEP, STEP)
-    factor = jnp.concatenate([factor_ref[b : b + 1, :] for b in range(blocks)], axis=1)
-    ratios = normed_ref[pl.ds(start, SPAN), :] * factor
-    level = pltpu.roll(ratios, SIDE, 1, stride=1, stride_axis=0)
-    stacked = jnp.concatenate(halves(level), axis=0)
-    summed = jnp.dot(down_table[...], stacked, preferred_element_type=jnp.float32)
-
-    def sideways(k):
-        parts = []
-        for half in halves(summed[k * STEP : (k + 1) * STEP, :]):
-            around = jnp.concatenate([half, half[:, :LANE]], axis=1)
-            parts.append(jnp.concatenate([around[:, b * LANE : (b + 2) * LANE] for b in range(blocks)], axis=0))
-        table = side_table[k]
-        result = jnp.dot(parts[0], table, preferred_element_type=jnp.float32)
-        return result + jnp.dot(parts[1], table, preferred_element_type=jnp.float32)
-
+    out_row = lax.broadcasted_iota(jnp.int32, (STEP, 2 * SPAN), 0)
+    out_row = (out_row // 8) * 8 + 7 - lax.rem(out_row, 8)
+    in_row = lax.broadcasted_iota(jnp.int32, (STEP, 2 * SPAN), 1)
+    in_row = jnp.where(in_row < SPAN, in_row, in_row - SPAN)
+    a = in_row - TOP - out_row
+    down_table = jnp.concatenate(
+        [
+            both(near(a, P_SIZE + 1, W), near(a, -W, -P_SIZE - 1)),
+            both(near(a, 1, P_SIZE), near(a, -P_SIZE, -1)),
+            both(near(a, P_SIZE + 1, W), near(a, P_SIZE + 1, W)),
+            both(near(a, 1, P_SIZE), near(a, 1, P_SIZE)),
+        ],
+        axis=0,
+    )
+    shape = (2 * LANE, LANE)
+    b = lax.broadcasted_iota(jnp.int32, shape, 0) - SIDE - lax.broadcasted_iota(jnp.int32, shape, 1)
+    side_table = [
+        both(near(b, 1, W), near(b, -W, -1)),
+        both(near(b, P_SIZE + 1, W), near(b, -W, -P_SIZE - 1)),
+        both(near(b, -W, -1), near(b, -W, -1)),
+        both(near(b, -W, -P_SIZE - 1), near(b, -W, -P_SIZE - 1)),
+    ]
     flip = 7 - lax.broadcasted_iota(jnp.int32, (8, cols), 0)
-    here = ratios[TOP : TOP + STEP, :cols]
     cells_donut = (2 * W + 1) ** 2 - (2 * P_SIZE + 1) ** 2 - 4 * (W - P_SIZE)
     cells_lower = W * W - P_SIZE * P_SIZE
-    for out_ref, k, cell_count in ((donut_ref, 0, cells_donut), (lower_ref, 2, cells_lower)):
-        tall = sideways(k) + sideways(k + 1)
-        flat = jnp.concatenate([tall[b * STEP : (b + 1) * STEP, :] for b in range(blocks)], axis=1)
-        for g in range(STEP // 8):
-            rows_g = slice(8 * g, 8 * g + 8)
-            back = pltpu.roll(flat[rows_g, :], width - TOP - 8 * g - 7, 1, stride=1, stride_axis=0)[:, :cols]
-            back = jnp.take_along_axis(back, flip, axis=0)
-            out_ref[rows_g, :] = here[rows_g, :] / jnp.maximum(back / cell_count, 0.25)
+    factor = jnp.concatenate([factor_ref[b : b + 1, :] for b in range(blocks)], axis=1)
+
+    copies = []
+    for start in range(0, rows, STEP):
+        ratios = normed_ref[start : start + SPAN, :] * factor
+        level = pltpu.roll(ratios, SIDE, 1, stride=1, stride_axis=0)
+        stacked = jnp.concatenate(halves(level), axis=0)
+        summed = jnp.dot(down_table, stacked, preferred_element_type=jnp.float32)
+
+        def sideways(k):
+            parts = []
+            for half in halves(summed[k * STEP : (k + 1) * STEP, :]):
+                around = jnp.concatenate([half, half[:, :LANE]], axis=1)
+                parts.append(jnp.concatenate([around[:, b * LANE : (b + 2) * LANE] for b in range(blocks)], axis=0))
+            return parts
+
+        here = ratios[TOP : TOP + STEP, :cols]
+        for to, out_ref, out, k, cell_count in (
+            (0, donut_ref, donut, 0, cells_donut),
+            (1, lower_ref, lower, 2, cells_lower),
+        ):
+            wide = jnp.concatenate(sideways(k) + sideways(k + 1), axis=1)
+            table = jnp.concatenate([side_table[k]] * 2 + [side_table[k + 1]] * 2, axis=0)
+            tall = jnp.dot(wide, table, preferred_element_type=jnp.float32)
+            flat = jnp.concatenate([tall[b * STEP : (b + 1) * STEP, :] for b in range(blocks)], axis=1)
+            for g in range(STEP // 8):
+                rows_g = slice(8 * g, 8 * g + 8)
+                back = pltpu.roll(flat[rows_g, :], width - TOP - 8 * g - 7, 1, stride=1, stride_axis=0)[:, :cols]
+                back = jnp.take_along_axis(back, flip, axis=0)
+                out[start + 8 * g : start + 8 * g + 8, :] = here[rows_g, :] / jnp.maximum(back / cell_count, 0.25)
+            span = pl.ds(start, STEP)
+            copies.append(pltpu.make_async_copy(out.at[span, :], out_ref.at[span, :], sems.at[to, start // STEP]))
+            copies[-1].start()
+    for copy in copies:
+        copy.wait()
+
+
+def windows(normed, factor):
+    rows, cols = normed.shape[0] - 2 * TOP, normed.shape[1] - LANE
+    out = jax.ShapeDtypeStruct((rows, cols), jnp.float32)
+    return pl.pallas_call(
+        window_kernel,
+        out_shape=(out, out),
+        in_specs=[pl.BlockSpec(memory_space=pltpu.VMEM), pl.BlockSpec(memory_space=pltpu.VMEM)],
+        out_specs=(pl.BlockSpec(memory_space=pltpu.HBM), pl.BlockSpec(memory_space=pltpu.HBM)),
+        scratch_shapes=[
+            pltpu.VMEM((rows, cols), jnp.float32),
+            pltpu.VMEM((rows, cols), jnp.float32),
+            pltpu.SemaphoreType.DMA((2, rows // STEP)),
+        ],
+        compiler_params=pltpu.CompilerParams(vmem_limit_bytes=32 * 1024 * 1024),
+        name="windows",
+    )(normed, factor)
 
 
 def local(counts, bin_mask):
@@ -460,20 +493,7 @@
         pltpu.with_memory_space_constraint(counts, pltpu.HBM),
         pltpu.with_memory_space_constraint(bin_mask.reshape(halves_n, LANE), pltpu.HBM),
     )
-    out = jax.ShapeDtypeStruct((rows, cols), jnp.float32)
-    return pl.pallas_call(
-        window_kernel,
-        grid=(rows // STEP,),
-        out_shape=(out, out),
-        in_specs=[pl.BlockSpec(memory_space=pltpu.VMEM), pl.BlockSpec(memory_space=pltpu.VMEM)],
-        out_specs=(pl.BlockSpec((STEP, cols), lambda i: (i, 0)), pl.BlockSpec((STEP, cols), lambda i: (i, 0))),
-        scratch_shapes=[
-            pltpu.VMEM((4 * STEP, 2 * SPAN), jnp.bfloat16),
-            pltpu.VMEM((4, 2 * LANE, LANE), jnp.bfloat16),
-        ],
-        compiler_params=pltpu.CompilerParams(vmem_limit_bytes=24 * 1024 * 1024),
-        name="windows",
-    )(normed, factor)
+    return windows(normed, factor)
 
 
 def solution(mesh):

time: 40.1 us -> 39.1 us (0.975)
  Pallas kernels: 39.3 us -> 38.4 us
    pallas_call x1, Pallas kernels: 5.64 us -> 4.43 us  [windows(): pl.pallas_call(window_kernel, out_shape=(out, out), in_specs=[pl.BlockSpe...]
where the time goes in v4:
time: 39.1 us; the launch traced here: 39 us
  Pallas kernels  38.4 us (98%)
  between operations  0.64 us (2%)
    pallas_call x1, Pallas kernels, local(): pl.pallas_call(functools.partial(comm_kernel, (n_pos, n_off)), out_shape=...  33.9 us
    pallas_call x1, Pallas kernels, windows(): pl.pallas_call(window_kernel, out_shape=(out, out), in_specs=[pl.BlockSpe...  4.43 us

profile of v4, /device:TPU:1, one launch (start us, length us, event | category | flops | bytes accessed | tf_op | source)
XLA Modules:
  0.0 39.0 jit_solution(5313238139410262518)
XLA Ops:
  0.6 33.9 %comm.1 = (f32[304,1152]{1,0:T(8,128)S(1)}, f32[9,128]{1,0:T(8,128)S(1)}) custom-call(f32[256,1024]{1,0:T(8,128)} %counts_ref.1, s32[2,128]{1,0:T(2,128)} %bitcast.1), custom_call_target="tpu_custom_call" | custom-call | tf_op jit(solution)/shard_map/comm/pallas_call | solution.py:454
  34.6 4.4 %windows.1 = (f32[256,1024]{1,0:T(8,128)}, f32[256,1024]{1,0:T(8,128)}) custom-call(f32[304,1152]{1,0:T(8,128)S(1)} %get-tuple-element.4.normed_ref, f32[9,128]{1,0:T(8,128)S(1)} %get-tuple-element.5.factor_ref), custom_call_target="tpu_custom_call" | custom-call | tf_op jit(solution)/shard_map/windows/pallas_call | solution.py:423

commit v5 on v4

--- a/solution.py
+++ b/solution.py
@@ -19,8 +19,9 @@
 
 def comm_kernel(
     sizes, counts_ref, mask_ref, normed_ref, factor_ref,
-    cells, strips_out, strips_in, mask, cov, own, wts, lines, row_w, tables, part, group,
-    load_sem, mask_sem, cov_send, cov_recv, halo_send, halo_recv, wts_send, wts_recv, part_send, part_recv, group_send, group_recv,
+    cells, strips_out, strips_in, mask, own_live, live, cov, own, wts, lines, row_w, tables, part, group, part_live, group_live,
+    load_sem, mask_sem, cov_send, cov_recv, halo_send, halo_recv, live_send, live_recv, wts_send, wts_recv,
+    part_send, part_recv, group_send, group_recv, part_live_send, part_live_recv, group_live_send, group_live_recv,
 ):
     n_pos, n_off = sizes
     rows, cols = counts_ref.shape
@@ -124,6 +125,7 @@
         turned = acc[h * LANE : (h + 1) * LANE, :].T
         cov[0, h : h + 1, :] = jnp.sum(turned, axis=0, keepdims=True)
     load_mask.wait()
+    own_live[...] = mask[...].astype(jnp.float32)
 
     n_greet = len(cov_peers) + len(moves) - 1 + len(halo_moves) + len(part_peers) + len(group_peers)
     pl.semaphore_wait(barrier, n_greet + jnp.where(off > 0, 1, 0))
@@ -138,6 +140,23 @@
     ]
     for copy in cov_copies:
         copy.start()
+
+    live_copies = [
+        remote(own_live, live.at[k], live_send.at[k], live_recv.at[k], wts_target(0, k)) for k in range(n_steps)
+    ]
+
+    def each_live(act):
+        for k, copy in enumerate(live_copies):
+            if k == self_step:
+                pl.when(off > 0)(getattr(copy, act))
+            else:
+                getattr(copy, act)()
+
+    each_live("start")
+
+    @pl.when(off == 0)
+    def _():
+        live[self_step] = own_live[...]
 
     spans = {-1: (pl.ds(0, TOP), pl.ds(TOP + rows, TOP)), 1: (pl.ds(rows - TOP, TOP), pl.ds(0, TOP))}
     strips = {
@@ -196,7 +215,7 @@
     for r in range(1, near_offs):
         coverage = coverage + cov[r]
     own[0:row_halves, :] = coverage
-    own[row_halves:, :] = mask[...].astype(jnp.float32)
+    own[row_halves:, :] = own_live[...]
 
     wts_copies = [
         remote(own, wts.at[t, slot], wts_send.at[t, slot], wts_recv.at[t, slot], wts_target(t, slot))
@@ -217,48 +236,92 @@
     def _():
         wts[0, self_step] = own[...]
 
+    def down(vector):
+        return jnp.broadcast_to(vector, (LANE, LANE)).T
+
+    phases = LANE // 8
+
+    def spread(source):
+        pieces = []
+        for k, d in enumerate(steps):
+            block = pos + first + d
+            inside = (block >= 0) & (block < n_pos)
+            for h in range(row_halves):
+                pieces.append(jnp.where(inside, source[k, h : h + 1, :], 0.0))
+        line = jnp.concatenate(pieces, axis=1)
+        reach = line.shape[1]
+        line = jnp.broadcast_to(line, (8, reach))
+        line = pltpu.roll(line, reach - 7, 1, stride=1, stride_axis=0)
+        flip = 7 - lax.broadcasted_iota(jnp.int32, (8, reach), 0)
+        line = jnp.take_along_axis(line, flip, axis=0)
+        for h in range(phases):
+            tables[h] = line if h == 0 else pltpu.roll(line, reach - 8 * h, 1)
+
+    lane_8 = lax.broadcasted_iota(jnp.int32, (8, LANE), 1)
+    low_lanes = lane_8 < SIDE
+
+    def column(g, b):
+        place = 8 * g + rows - TOP
+        h, shift = (place % LANE) // 8, place // LANE * LANE
+        if b < blocks:
+            return tables[h, :, shift + b * LANE : shift + (b + 1) * LANE]
+        after = tables[h, :, shift + cols : shift + cols + LANE]
+        return jnp.where(low_lanes, after, tables[h, :, shift - LANE : shift])
+
+    own_groups = range(TOP // 8, (TOP + rows) // 8)
+
+    def column_sums(to, terms_of):
+        sums = [None] * (blocks + 1)
+        for g in own_groups:
+            for b, term in enumerate(terms_of(g)):
+                sums[b] = term if sums[b] is None else sums[b] + term
+        for b, total in enumerate(sums):
+            to[0, b : b + 1, :] = jnp.sum(total, axis=0, keepdims=True)
+
+    def share(buffer, send, recv, peers):
+        copies = [
+            remote(buffer.at[0], buffer.at[r], send.at[r], recv.at[r], peers[r - 1]) for r in range(1, buffer.shape[0])
+        ]
+        for copy in copies:
+            copy.start()
+        return copies
+
+    def gather(copies, buffer):
+        for copy in copies:
+            copy.wait_recv()
+        total = buffer[0]
+        for r in range(1, buffer.shape[0]):
+            total = total + buffer[r]
+        return total
+
+    each_live("wait_recv")
+    for h in range(row_halves):
+        row_w[TOP + h * LANE : TOP + (h + 1) * LANE, :] = down(own_live[h : h + 1, :])
+    spread(live)
+
+    def live_terms(g):
+        row = row_w[8 * g : 8 * g + 8, :]
+        return [row * column(g, b) for b in range(blocks + 1)]
+
+    column_sums(part_live, live_terms)
+    part_live_copies = share(part_live, part_live_send, part_live_recv, part_peers)
+
     each_wts("wait_recv")
-
     gathered = wts[0, :, 0:row_halves, :]
     for t in range(1, far_offs):
         gathered = gathered + wts[t, :, 0:row_halves, :]
     lines[...] = wts[0, :, row_halves:, :] / jnp.sqrt(gathered)
-
-    def down(vector):
-        return jnp.broadcast_to(vector, (LANE, LANE)).T
-
     for h in range(row_halves):
         row_w[TOP + h * LANE : TOP + (h + 1) * LANE, :] = down(lines[n_slots - 1, h : h + 1, :])
-
-    pieces = []
-    for k, d in enumerate(steps):
-        block = pos + first + d
-        inside = (block >= 0) & (block < n_pos)
-        for h in range(row_halves):
-            pieces.append(jnp.where(inside, lines[k, h : h + 1, :], 0.0))
-    line = jnp.concatenate(pieces, axis=1)
-    reach = line.shape[1]
-    line = jnp.broadcast_to(line, (8, reach))
-    line = pltpu.roll(line, reach - 7, 1, stride=1, stride_axis=0)
-    flip = 7 - lax.broadcasted_iota(jnp.int32, (8, reach), 0)
-    line = jnp.take_along_axis(line, flip, axis=0)
-    phases = LANE // 8
-    for h in range(phases):
-        tables[h] = line if h == 0 else pltpu.roll(line, reach - 8 * h, 1)
-
-    lane_8 = lax.broadcasted_iota(jnp.int32, (8, LANE), 1)
-    low_lanes = lane_8 < SIDE
+    spread(lines)
 
     def row_group(g):
         rows_g = slice(8 * g, 8 * g + 8)
-        place = 8 * g + rows - TOP
-        h, shift = (place % LANE) // 8, place // LANE * LANE
         weight = row_w[rows_g, :]
         outs = []
         for b in range(blocks + 1):
             if b < blocks:
                 count = cells[rows_g, b * LANE : (b + 1) * LANE]
-                col = tables[h, :, shift + b * LANE : shift + (b + 1) * LANE]
             else:
                 own_row = 8 * g - TOP
                 if 0 <= own_row < rows:
@@ -270,30 +333,14 @@
                 else:
                     after, before = cells[rows_g, cols : cols + LANE], cells[rows_g, cols + LANE : cols + 2 * LANE]
                 count = jnp.where(low_lanes, after, before)
-                col = jnp.where(
-                    low_lanes,
-                    tables[h, :, shift + cols : shift + cols + LANE],
-                    tables[h, :, shift - LANE : shift],
-                )
-            value = count * weight * col
+            value = count * weight * column(g, b)
             normed_ref[rows_g, b * LANE : (b + 1) * LANE] = value
-            outs.append((value, jnp.where((weight > 0) & (col > 0), 1.0, 0.0)))
+            outs.append(value)
         return outs
 
     each_halo(halos[:2], "wait_recv")
-    sums = [None] * (2 * (blocks + 1))
-    for g in range(TOP // 8, (TOP + rows) // 8):
-        for b, (value, live) in enumerate(row_group(g)):
-            for k, term in ((b, value), (blocks + 1 + b, live)):
-                sums[k] = term if sums[k] is None else sums[k] + term
-    for k, total in enumerate(sums):
-        part[0, k : k + 1, :] = jnp.sum(total, axis=0, keepdims=True)
-
-    part_copies = [
-        remote(part.at[0], part.at[r], part_send.at[r], part_recv.at[r], part_peers[r - 1]) for r in range(1, inner)
-    ]
-    for copy in part_copies:
-        copy.start()
+    column_sums(part, row_group)
+    part_copies = share(part, part_send, part_recv, part_peers)
 
     each_halo(halos[2:], "wait_recv")
     for side, h, low, place in ((0, row_halves - 1, LANE - TOP, 0), (1, 0, 0, TOP + rows)):
@@ -304,36 +351,24 @@
     for g in list(range(TOP // 8)) + list(range((TOP + rows) // 8, (2 * TOP + rows) // 8)):
         row_group(g)
 
-    for copy in part_copies:
-        copy.wait_recv()
-    total = part[0]
-    for r in range(1, inner):
-        total = total + part[r]
-    group[0] = total
-    group_copies = [
-        remote(group.at[0], group.at[r], group_send.at[r], group_recv.at[r], group_peers[r - 1])
-        for r in range(1, outer)
-    ]
-    for copy in group_copies:
-        copy.start()
-    for copy in cov_copies + part_copies:
+    group_live[0] = gather(part_live_copies, part_live)
+    group_live_copies = share(group_live, group_live_send, group_live_recv, group_peers)
+    group[0] = gather(part_copies, part)
+    group_copies = share(group, group_send, group_recv, group_peers)
+    for copy in cov_copies + part_copies + part_live_copies:
         copy.wait_send()
     each_halo(halos, "wait_send")
     each_wts("wait_send")
-    for copy in group_copies:
-        copy.wait_recv()
-    total = group[0]
-    for r in range(1, outer):
-        total = total + group[r]
-    expected = total[: blocks + 1, :]
-    pairs = total[blocks + 1 :, :]
+    each_live("wait_send")
+    pairs = gather(group_live_copies, group_live)
+    expected = gather(group_copies, group)
     lane = lax.broadcasted_iota(jnp.int32, expected.shape, 1)
     place = lax.broadcasted_iota(jnp.int32, expected.shape, 0) * LANE + lane
     needed = (place < cols + 2 * W) | (place >= width - 2 * W)
     place = off * cols + jnp.where(place < cols + SIDE, place, place - width)
     factor = pairs / jnp.where(expected > 0, expected, 1.0)
     factor_ref[...] = jnp.where(needed & (place >= 0) & (place < band), factor, 0.0)
-    for copy in group_copies:
+    for copy in group_copies + group_live_copies:
         copy.wait_send()
 
 
@@ -369,42 +404,62 @@
         ],
         axis=0,
     )
-    shape = (2 * LANE, LANE)
-    b = lax.broadcasted_iota(jnp.int32, shape, 0) - SIDE - lax.broadcasted_iota(jnp.int32, shape, 1)
-    side_table = [
-        both(near(b, 1, W), near(b, -W, -1)),
-        both(near(b, P_SIZE + 1, W), near(b, -W, -P_SIZE - 1)),
-        both(near(b, -W, -1), near(b, -W, -1)),
-        both(near(b, -W, -P_SIZE - 1), near(b, -W, -P_SIZE - 1)),
-    ]
+    def side_tables(depth, wide, split):
+        shape = (depth, wide)
+        at = lax.broadcasted_iota(jnp.int32, shape, 0)
+        if split:
+            at = jnp.where(at < SIDE, at + wide, at - LANE)
+        b = at - lax.broadcasted_iota(jnp.int32, shape, 1)
+        return [
+            both(near(b, 1, W), near(b, -W, -1)),
+            both(near(b, P_SIZE + 1, W), near(b, -W, -P_SIZE - 1)),
+            both(near(b, -W, -1), near(b, -W, -1)),
+            both(near(b, -W, -P_SIZE - 1), near(b, -W, -P_SIZE - 1)),
+        ]
+
+    main_t, rim_t = side_tables(2 * LANE, 2 * LANE, False), side_tables(LANE, 2 * LANE, True)
+    mid_t, edge_t = side_tables(LANE, LANE, False), side_tables(LANE, LANE, True)
+    pair_table, last_table = [], []
+    for k in (0, 2):
+        pair_table.append(jnp.concatenate([main_t[k]] * 2 + [main_t[k + 1]] * 2 + [rim_t[k]] * 2 + [rim_t[k + 1]] * 2, axis=0))
+        last_table.append(jnp.concatenate([mid_t[k], edge_t[k]] * 2 + [mid_t[k + 1], edge_t[k + 1]] * 2, axis=0))
     flip = 7 - lax.broadcasted_iota(jnp.int32, (8, cols), 0)
     cells_donut = (2 * W + 1) ** 2 - (2 * P_SIZE + 1) ** 2 - 4 * (W - P_SIZE)
     cells_lower = W * W - P_SIZE * P_SIZE
     factor = jnp.concatenate([factor_ref[b : b + 1, :] for b in range(blocks)], axis=1)
 
     copies = []
-    for start in range(0, rows, STEP):
+
+    def upright(start):
         ratios = normed_ref[start : start + SPAN, :] * factor
-        level = pltpu.roll(ratios, SIDE, 1, stride=1, stride_axis=0)
+        level = pltpu.roll(ratios, 0, 1, stride=1, stride_axis=0)
         stacked = jnp.concatenate(halves(level), axis=0)
         summed = jnp.dot(down_table, stacked, preferred_element_type=jnp.float32)
-
-        def sideways(k):
-            parts = []
-            for half in halves(summed[k * STEP : (k + 1) * STEP, :]):
-                around = jnp.concatenate([half, half[:, :LANE]], axis=1)
-                parts.append(jnp.concatenate([around[:, b * LANE : (b + 2) * LANE] for b in range(blocks)], axis=0))
-            return parts
-
-        here = ratios[TOP : TOP + STEP, :cols]
+        return ratios[TOP : TOP + STEP, :cols], summed
+
+    lanes = lax.broadcasted_iota(jnp.int32, (STEP, LANE), 1)
+
+    def sideways(summed, k):
+        mains, rims = [], []
+        x = summed[k * STEP : (k + 1) * STEP, :]
+        pieces = [x[:, b * LANE : (b + 1) * LANE] for b in range(blocks)]
+        rim = jnp.concatenate(
+            [jnp.where(lanes < SIDE, pieces[(2 * c + 2) % blocks], pieces[(2 * c - 1) % blocks]) for c in range(blocks // 2)],
+            axis=0,
+        )
+        last = jnp.concatenate([pieces[-1], jnp.where(lanes < SIDE, pieces[0], pieces[-2])], axis=1)
+        main = jnp.concatenate([x[:, 2 * c * LANE : (2 * c + 2) * LANE] for c in range(blocks // 2)], axis=0)
+        return halves(main), halves(rim), halves(last)
+
+    def level_out(start, here, summed):
         for to, out_ref, out, k, cell_count in (
             (0, donut_ref, donut, 0, cells_donut),
             (1, lower_ref, lower, 2, cells_lower),
         ):
-            wide = jnp.concatenate(sideways(k) + sideways(k + 1), axis=1)
-            table = jnp.concatenate([side_table[k]] * 2 + [side_table[k + 1]] * 2, axis=0)
-            tall = jnp.dot(wide, table, preferred_element_type=jnp.float32)
-            flat = jnp.concatenate([tall[b * STEP : (b + 1) * STEP, :] for b in range(blocks)], axis=1)
+            (m0, r0, l0), (m1, r1, l1) = sideways(summed, k), sideways(summed, k + 1)
+            tall = jnp.dot(jnp.concatenate(m0 + m1 + r0 + r1, axis=1), pair_table[k // 2], preferred_element_type=jnp.float32)
+            end = jnp.dot(jnp.concatenate(l0 + l1, axis=1), last_table[k // 2], preferred_element_type=jnp.float32)
+            flat = jnp.concatenate([tall[c * STEP : (c + 1) * STEP, :] for c in range(blocks // 2)] + [end], axis=1)
             for g in range(STEP // 8):
                 rows_g = slice(8 * g, 8 * g + 8)
                 back = pltpu.roll(flat[rows_g, :], width - TOP - 8 * g - 7, 1, stride=1, stride_axis=0)[:, :cols]
@@ -413,6 +468,9 @@
             span = pl.ds(start, STEP)
             copies.append(pltpu.make_async_copy(out.at[span, :], out_ref.at[span, :], sems.at[to, start // STEP]))
             copies[-1].start()
+
+    for start in range(0, rows, STEP):
+        level_out(start, *upright(start))
     for copy in copies:
         copy.wait()
 
@@ -444,7 +502,7 @@
     near_offs = 4
     far_offs = n_off // near_offs
     width = cols + LANE
-    vecs = 2 * (cols // LANE + 1)
+    vecs = cols // LANE + 1
     n_slots = cols // rows + 6
     reach = (cols // rows + 3) * rows
     halves_n = rows // LANE
@@ -455,7 +513,7 @@
         functools.partial(comm_kernel, (n_pos, n_off)),
         out_shape=(
             pltpu.VMEM((rows + 2 * TOP, width), f32),
-            pltpu.VMEM((vecs // 2, LANE), f32),
+            pltpu.VMEM((vecs, LANE), f32),
         ),
         in_specs=[pl.BlockSpec(memory_space=pltpu.HBM), pl.BlockSpec(memory_space=pltpu.HBM)],
         out_specs=(pl.BlockSpec(memory_space=pltpu.VMEM), pl.BlockSpec(memory_space=pltpu.VMEM)),
@@ -464,6 +522,8 @@
             pltpu.VMEM((2, third, LANE), f32),
             pltpu.VMEM((2, third, LANE), f32),
             pltpu.VMEM((halves_n, LANE), jnp.int32),
+            pltpu.VMEM((halves_n, LANE), f32),
+            pltpu.VMEM((n_slots - 3, halves_n, LANE), f32),
             pltpu.VMEM((near_offs, halves_n, LANE), f32),
             pltpu.VMEM((2 * halves_n, LANE), f32),
             pltpu.VMEM((far_offs, n_slots, 2 * halves_n, LANE), f32),
@@ -472,14 +532,22 @@
             pltpu.VMEM((LANE // 8, 8, reach), f32),
             pltpu.VMEM((inner, vecs, LANE), f32),
             pltpu.VMEM((outer, vecs, LANE), f32),
+            pltpu.VMEM((inner, vecs, LANE), f32),
+            pltpu.VMEM((outer, vecs, LANE), f32),
             dma,
             dma,
             dma((near_offs,)),
             dma((near_offs,)),
             dma((8,)),
             dma((8,)),
+            dma((n_slots - 3,)),
+            dma((n_slots - 3,)),
             dma((far_offs, n_slots)),
             dma((far_offs, n_slots)),
+            dma((inner,)),
+            dma((inner,)),
+            dma((outer,)),
+            dma((outer,)),
             dma((inner,)),
             dma((inner,)),
             dma((outer,)),

time: 39.1 us -> 38.9 us (level)
  no operation moved by 1% of the time
where the time goes in v5:
time: 38.9 us; the launch traced here: 38.8 us
  Pallas kernels  38.1 us (98%)
  between operations  0.64 us (2%)
    pallas_call x1, Pallas kernels, local(): pl.pallas_call(functools.partial(comm_kernel, (n_pos, n_off)), out_shape=...  33.9 us
    pallas_call x1, Pallas kernels, windows(): pl.pallas_call(window_kernel, out_shape=(out, out), in_specs=[pl.BlockSpe...  4.26 us

profile of v5, /device:TPU:1, one launch (start us, length us, event | category | flops | bytes accessed | tf_op | source)
XLA Modules:
  0.0 38.8 jit_solution(5538356562590985912)
XLA Ops:
  0.6 33.9 %comm.1 = (f32[304,1152]{1,0:T(8,128)S(1)}, f32[9,128]{1,0:T(8,128)S(1)}) custom-call(f32[256,1024]{1,0:T(8,128)} %counts_ref.1, s32[2,128]{1,0:T(2,128)} %bitcast.1), custom_call_target="tpu_custom_call" | custom-call | tf_op jit(solution)/shard_map/comm/pallas_call | solution.py:512
  34.5 4.3 %windows.1 = (f32[256,1024]{1,0:T(8,128)}, f32[256,1024]{1,0:T(8,128)}) custom-call(f32[304,1152]{1,0:T(8,128)S(1)} %get-tuple-element.4.normed_ref, f32[9,128]{1,0:T(8,128)S(1)} %get-tuple-element.5.factor_ref), custom_call_target="tpu_custom_call" | custom-call | tf_op jit(solution)/shard_map/windows/pallas_call | solution.py:481

commit v6 on v5

--- a/solution.py
+++ b/solution.py
@@ -55,6 +55,7 @@
     steps = list(range(-1, ratio + 2))
     n_steps = len(steps)
     self_step = steps.index(0)
+    own_slot = n_steps
     n_slots = n_steps + 3
     part_peers = [(quot * inner + lax.rem(rank + r, inner), off) for r in range(1, inner)]
     group_peers = [(lax.rem(quot + r, outer) * inner + rank, off) for r in range(1, outer)]
@@ -63,19 +64,20 @@
         there = lax.rem(far + t, far_offs) * near_offs + near
         if slot < n_steps:
             return (lax.rem(pos - ratio * there - steps[slot] + n_pos, n_pos), there)
-        return (at_pos((1, -1, 0)[slot - n_steps]), there)
+        return (at_pos((0, 1, -1)[slot - n_steps]), there)
 
     def wts_source(t, slot):
         there = lax.rem(far - t + far_offs, far_offs) * near_offs + near
         if slot < n_steps:
             return (lax.rem(pos + first + steps[slot] + n_pos, n_pos), there)
-        return (at_pos((-1, 1, 0)[slot - n_steps]), there)
+        return (at_pos((0, -1, 1)[slot - n_steps]), there)
 
     moves = []
     for t in list(range(1, far_offs)) + [0]:
         for slot in range(n_slots):
-            if t or slot != n_slots - 1:
+            if t or slot != own_slot:
                 moves.append((t, slot, t == 0 and slot == self_step))
+    live_slots = [slot for slot in range(n_slots) if slot != own_slot]
 
     load = pltpu.make_async_copy(counts_ref, cells.at[pl.ds(TOP, rows), pl.ds(0, cols)], load_sem)
     load.start()
@@ -87,13 +89,13 @@
     def greet(device):
         pl.semaphore_signal(barrier, inc=1, device_id=device, device_id_type=MESH)
 
-    for device in cov_peers:
-        greet(device)
     for t, slot, selfish in moves:
         if selfish:
             pl.when(off > 0)(functools.partial(greet, wts_source(t, slot)))
         else:
             greet(wts_source(t, slot))
+    for device in cov_peers:
+        greet(device)
     for a, b in halo_moves:
         greet((at_pos(-a), at_off(-b)))
     for device in part_peers + group_peers:
@@ -142,17 +144,18 @@
         copy.start()
 
     live_copies = [
-        remote(own_live, live.at[k], live_send.at[k], live_recv.at[k], wts_target(0, k)) for k in range(n_steps)
+        remote(own_live, live.at[k], live_send.at[k], live_recv.at[k], wts_target(0, k)) for k in live_slots
     ]
 
     def each_live(act):
-        for k, copy in enumerate(live_copies):
+        for k, copy in zip(live_slots, live_copies):
             if k == self_step:
                 pl.when(off > 0)(getattr(copy, act))
             else:
                 getattr(copy, act)()
 
     each_live("start")
+    live[own_slot] = own_live[...]
 
     @pl.when(off == 0)
     def _():
@@ -214,23 +217,24 @@
     coverage = cov[0]
     for r in range(1, near_offs):
         coverage = coverage + cov[r]
-    own[0:row_halves, :] = coverage
-    own[row_halves:, :] = own_live[...]
+    own[...] = coverage
 
     wts_copies = [
         remote(own, wts.at[t, slot], wts_send.at[t, slot], wts_recv.at[t, slot], wts_target(t, slot))
         for t, slot, _ in moves
     ]
 
-    def each_wts(act):
-        for (_, _, selfish), copy in zip(moves, wts_copies):
+    def each_wts(act, side):
+        for (_, slot, selfish), copy in zip(moves, wts_copies):
+            if side != (slot > own_slot):
+                continue
             if selfish:
                 pl.when(off > 0)(getattr(copy, act))
             else:
                 getattr(copy, act)()
 
-    each_wts("start")
-    wts[0, n_slots - 1] = own[...]
+    each_wts("start", False)
+    wts[0, own_slot] = own[...]
 
     @pl.when(off == 0)
     def _():
@@ -306,13 +310,16 @@
     column_sums(part_live, live_terms)
     part_live_copies = share(part_live, part_live_send, part_live_recv, part_peers)
 
-    each_wts("wait_recv")
-    gathered = wts[0, :, 0:row_halves, :]
-    for t in range(1, far_offs):
-        gathered = gathered + wts[t, :, 0:row_halves, :]
-    lines[...] = wts[0, :, row_halves:, :] / jnp.sqrt(gathered)
+    def weigh(low, high):
+        gathered = wts[0, low:high]
+        for t in range(1, far_offs):
+            gathered = gathered + wts[t, low:high]
+        lines[low:high] = live[low:high] / jnp.sqrt(gathered)
+
+    each_wts("wait_recv", False)
+    weigh(0, own_slot + 1)
     for h in range(row_halves):
-        row_w[TOP + h * LANE : TOP + (h + 1) * LANE, :] = down(lines[n_slots - 1, h : h + 1, :])
+        row_w[TOP + h * LANE : TOP + (h + 1) * LANE, :] = down(lines[own_slot, h : h + 1, :])
     spread(lines)
 
     def row_group(g):
@@ -342,23 +349,29 @@
     column_sums(part, row_group)
     part_copies = share(part, part_send, part_recv, part_peers)
 
-    each_halo(halos[2:], "wait_recv")
-    for side, h, low, place in ((0, row_halves - 1, LANE - TOP, 0), (1, 0, 0, TOP + rows)):
-        block = pos + (1 if side else -1)
-        inside = (block >= 0) & (block < n_pos)
-        weight = jnp.where(inside, lines[n_steps + side, h : h + 1, :], 0.0)
-        row_w[place : place + TOP, :] = down(weight)[low : low + TOP, :]
-    for g in list(range(TOP // 8)) + list(range((TOP + rows) // 8, (2 * TOP + rows) // 8)):
-        row_group(g)
+    each_wts("start", True)
 
     group_live[0] = gather(part_live_copies, part_live)
     group_live_copies = share(group_live, group_live_send, group_live_recv, group_peers)
     group[0] = gather(part_copies, part)
     group_copies = share(group, group_send, group_recv, group_peers)
+
+    each_halo(halos[2:], "wait_recv")
+    each_wts("wait_recv", True)
+    weigh(own_slot + 1, n_slots)
+    for side, h, low, place in ((0, row_halves - 1, LANE - TOP, 0), (1, 0, 0, TOP + rows)):
+        block = pos + (1 if side else -1)
+        inside = (block >= 0) & (block < n_pos)
+        weight = jnp.where(inside, lines[own_slot + 1 + side, h : h + 1, :], 0.0)
+        row_w[place : place + TOP, :] = down(weight)[low : low + TOP, :]
+    for g in list(range(TOP // 8)) + list(range((TOP + rows) // 8, (2 * TOP + rows) // 8)):
+        row_group(g)
+
     for copy in cov_copies + part_copies + part_live_copies:
         copy.wait_send()
     each_halo(halos, "wait_send")
-    each_wts("wait_send")
+    each_wts("wait_send", False)
+    each_wts("wait_send", True)
     each_live("wait_send")
     pairs = gather(group_live_copies, group_live)
     expected = gather(group_copies, group)
@@ -523,10 +536,10 @@
             pltpu.VMEM((2, third, LANE), f32),
             pltpu.VMEM((halves_n, LANE), jnp.int32),
             pltpu.VMEM((halves_n, LANE), f32),
-            pltpu.VMEM((n_slots - 3, halves_n, LANE), f32),
+            pltpu.VMEM((n_slots, halves_n, LANE), f32),
             pltpu.VMEM((near_offs, halves_n, LANE), f32),
-            pltpu.VMEM((2 * halves_n, LANE), f32),
-            pltpu.VMEM((far_offs, n_slots, 2 * halves_n, LANE), f32),
+            pltpu.VMEM((halves_n, LANE), f32),
+            pltpu.VMEM((far_offs, n_slots, halves_n, LANE), f32),
             pltpu.VMEM((n_slots, halves_n, LANE), f32),
             pltpu.VMEM((rows + 2 * TOP, LANE), f32),
             pltpu.VMEM((LANE // 8, 8, reach), f32),
@@ -540,8 +553,8 @@
             dma((near_offs,)),
             dma((8,)),
             dma((8,)),
-            dma((n_slots - 3,)),
-            dma((n_slots - 3,)),
+            dma((n_slots,)),
+            dma((n_slots,)),
             dma((far_offs, n_slots)),
             dma((far_offs, n_slots)),
             dma((inner,)),

time: 38.9 us -> 39 us (level)
  no operation moved by 1% of the time
where the time goes in v6:
time: 39 us; the launch traced here: 38.9 us
  Pallas kernels  38.3 us (98%)
  between operations  0.64 us (2%)
    pallas_call x1, Pallas kernels, local(): pl.pallas_call(functools.partial(comm_kernel, (n_pos, n_off)), out_shape=...  34 us
    pallas_call x1, Pallas kernels, windows(): pl.pallas_call(window_kernel, out_shape=(out, out), in_specs=[pl.BlockSpe...  4.26 us

profile of v6, /device:TPU:1, one launch (start us, length us, event | category | flops | bytes accessed | tf_op | source)
XLA Modules:
  0.0 38.9 jit_solution(15806125523048201113)
XLA Ops:
  0.6 34.0 %comm.1 = (f32[304,1152]{1,0:T(8,128)S(1)}, f32[9,128]{1,0:T(8,128)S(1)}) custom-call(f32[256,1024]{1,0:T(8,128)} %counts_ref.1, s32[2,128]{1,0:T(2,128)} %bitcast.1), custom_call_target="tpu_custom_call" | custom-call | tf_op jit(solution)/shard_map/comm/pallas_call | solution.py:525
  34.6 4.3 %windows.1 = (f32[256,1024]{1,0:T(8,128)}, f32[256,1024]{1,0:T(8,128)}) custom-call(f32[304,1152]{1,0:T(8,128)S(1)} %get-tuple-element.4.normed_ref, f32[9,128]{1,0:T(8,128)S(1)} %get-tuple-element.5.factor_ref), custom_call_target="tpu_custom_call" | custom-call | tf_op jit(solution)/shard_map/windows/pallas_call | solution.py:494

commit v7 on v6

--- a/solution.py
+++ b/solution.py
@@ -72,11 +72,27 @@
             return (lax.rem(pos + first + steps[slot] + n_pos, n_pos), there)
         return (at_pos((0, -1, 1)[slot - n_steps]), there)
 
+    def within(place):
+        return (place >= 0) & (place < n_pos)
+
+    def wts_sends(t, slot):
+        there = lax.rem(far + t, far_offs) * near_offs + near
+        if slot < n_steps:
+            valid = within(pos - ratio * there - steps[slot])
+            return valid & (off > 0) if t == 0 and slot == self_step else valid
+        return within(pos + (0, 1, -1)[slot - n_steps])
+
+    def wts_receives(t, slot):
+        if slot < n_steps:
+            valid = within(pos + first + steps[slot])
+            return valid & (off > 0) if t == 0 and slot == self_step else valid
+        return within(pos + (0, -1, 1)[slot - n_steps])
+
     moves = []
     for t in list(range(1, far_offs)) + [0]:
         for slot in range(n_slots):
             if t or slot != own_slot:
-                moves.append((t, slot, t == 0 and slot == self_step))
+                moves.append((t, slot))
     live_slots = [slot for slot in range(n_slots) if slot != own_slot]
 
     load = pltpu.make_async_copy(counts_ref, cells.at[pl.ds(TOP, rows), pl.ds(0, cols)], load_sem)
@@ -89,11 +105,11 @@
     def greet(device):
         pl.semaphore_signal(barrier, inc=1, device_id=device, device_id_type=MESH)
 
-    for t, slot, selfish in moves:
-        if selfish:
-            pl.when(off > 0)(functools.partial(greet, wts_source(t, slot)))
+    for t, slot in moves:
+        if slot == own_slot:
+            greet(wts_source(t, slot))
         else:
-            greet(wts_source(t, slot))
+            pl.when(wts_receives(t, slot))(functools.partial(greet, wts_source(t, slot)))
     for device in cov_peers:
         greet(device)
     for a, b in halo_moves:
@@ -129,8 +145,10 @@
     load_mask.wait()
     own_live[...] = mask[...].astype(jnp.float32)
 
-    n_greet = len(cov_peers) + len(moves) - 1 + len(halo_moves) + len(part_peers) + len(group_peers)
-    pl.semaphore_wait(barrier, n_greet + jnp.where(off > 0, 1, 0))
+    n_greet = len(cov_peers) + len(halo_moves) + len(part_peers) + len(group_peers)
+    for t, slot in moves:
+        n_greet = n_greet + jnp.where(wts_sends(t, slot), 1, 0)
+    pl.semaphore_wait(barrier, n_greet)
 
     def remote(src, dst, send, recv, device):
         return pltpu.make_async_remote_copy(
@@ -148,11 +166,9 @@
     ]
 
     def each_live(act):
+        valid = wts_receives if act == "wait_recv" else wts_sends
         for k, copy in zip(live_slots, live_copies):
-            if k == self_step:
-                pl.when(off > 0)(getattr(copy, act))
-            else:
-                getattr(copy, act)()
+            pl.when(valid(0, k))(getattr(copy, act))
 
     each_live("start")
     live[own_slot] = own_live[...]
@@ -221,17 +237,18 @@
 
     wts_copies = [
         remote(own, wts.at[t, slot], wts_send.at[t, slot], wts_recv.at[t, slot], wts_target(t, slot))
-        for t, slot, _ in moves
+        for t, slot in moves
     ]
 
     def each_wts(act, side):
-        for (_, slot, selfish), copy in zip(moves, wts_copies):
+        valid = wts_receives if act == "wait_recv" else wts_sends
+        for (t, slot), copy in zip(moves, wts_copies):
             if side != (slot > own_slot):
                 continue
-            if selfish:
-                pl.when(off > 0)(getattr(copy, act))
+            if slot == own_slot:
+                getattr(copy, act)()
             else:
-                getattr(copy, act)()
+                pl.when(valid(t, slot))(getattr(copy, act))
 
     each_wts("start", False)
     wts[0, own_slot] = own[...]

time: 39 us -> 38.1 us (0.977)
  Pallas kernels: 38.3 us -> 37.3 us
    pallas_call x1, Pallas kernels: 34 us -> 33 us  [local(): pl.pallas_call(functools.partial(comm_kernel, (n_pos, n_off)), out_shape=...]
where the time goes in v7:
time: 38.1 us; the launch traced here: 37.9 us
  Pallas kernels  37.3 us (98%)
  between operations  0.64 us (2%)
    pallas_call x1, Pallas kernels, local(): pl.pallas_call(functools.partial(comm_kernel, (n_pos, n_off)), out_shape=...  33 us
    pallas_call x1, Pallas kernels, windows(): pl.pallas_call(window_kernel, out_shape=(out, out), in_specs=[pl.BlockSpe...  4.25 us

profile of v7, /device:TPU:1, one launch (start us, length us, event | category | flops | bytes accessed | tf_op | source)
XLA Modules:
  0.0 37.9 jit_solution(14938264990858044832)
XLA Ops:
  0.6 33.0 %comm.1 = (f32[304,1152]{1,0:T(8,128)S(1)}, f32[9,128]{1,0:T(8,128)S(1)}) custom-call(f32[256,1024]{1,0:T(8,128)} %counts_ref.1, s32[2,128]{1,0:T(2,128)} %bitcast.1), custom_call_target="tpu_custom_call" | custom-call | tf_op jit(solution)/shard_map/comm/pallas_call | solution.py:542
  33.7 4.3 %windows.1 = (f32[256,1024]{1,0:T(8,128)}, f32[256,1024]{1,0:T(8,128)}) custom-call(f32[304,1152]{1,0:T(8,128)S(1)} %get-tuple-element.4.normed_ref, f32[9,128]{1,0:T(8,128)S(1)} %get-tuple-element.5.factor_ref), custom_call_target="tpu_custom_call" | custom-call | tf_op jit(solution)/shard_map/windows/pallas_call | solution.py:511

commit v8 on v7

--- a/solution.py
+++ b/solution.py
@@ -100,6 +100,9 @@
     load_mask = pltpu.make_async_copy(mask_ref, mask, mask_sem)
     load_mask.start()
 
+    def sends(b):
+        return off > 0 if b < 0 else off < n_off - 1
+
     barrier = pltpu.get_barrier_semaphore()
 
     def greet(device):
@@ -113,7 +116,11 @@
     for device in cov_peers:
         greet(device)
     for a, b in halo_moves:
-        greet((at_pos(-a), at_off(-b)))
+        source = (at_pos(-a), at_off(-b))
+        if b == 0:
+            greet(source)
+        else:
+            pl.when(sends(-b))(functools.partial(greet, source))
     for device in part_peers + group_peers:
         greet(device)
 
@@ -145,7 +152,9 @@
     load_mask.wait()
     own_live[...] = mask[...].astype(jnp.float32)
 
-    n_greet = len(cov_peers) + len(halo_moves) + len(part_peers) + len(group_peers)
+    n_greet = len(cov_peers) + len(part_peers) + len(group_peers)
+    for _, b in halo_moves:
+        n_greet = n_greet + (jnp.where(sends(b), 1, 0) if b else 1)
     for t, slot in moves:
         n_greet = n_greet + jnp.where(wts_sends(t, slot), 1, 0)
     pl.semaphore_wait(barrier, n_greet)
@@ -191,9 +200,6 @@
         else:
             ends = counts_ref.at[spans[a][0], strips[b][0]], cells.at[spans[a][1], strips[b][1]]
         halo_copies.append(remote(*ends, halo_send.at[k], halo_recv.at[k], (at_pos(a), at_off(b))))
-
-    def sends(b):
-        return off > 0 if b < 0 else off < n_off - 1
 
     def each_halo(copies, act):
         for (a, b), copy in copies:

time: 38.1 us -> 38 us (level)
  no operation moved by 1% of the time
where the time goes in v8:
time: 38 us; the launch traced here: 37.9 us
  Pallas kernels  37.2 us (98%)
  between operations  0.64 us (2%)
    pallas_call x1, Pallas kernels, local(): pl.pallas_call(functools.partial(comm_kernel, (n_pos, n_off)), out_shape=...  33 us
    pallas_call x1, Pallas kernels, windows(): pl.pallas_call(window_kernel, out_shape=(out, out), in_specs=[pl.BlockSpe...  4.25 us

profile of v8, /device:TPU:1, one launch (start us, length us, event | category | flops | bytes accessed | tf_op | source)
XLA Modules:
  0.0 37.9 jit_solution(5642206769936514810)
XLA Ops:
  0.6 33.0 %comm.1 = (f32[304,1152]{1,0:T(8,128)S(1)}, f32[9,128]{1,0:T(8,128)S(1)}) custom-call(f32[256,1024]{1,0:T(8,128)} %counts_ref.1, s32[2,128]{1,0:T(2,128)} %bitcast.1), custom_call_target="tpu_custom_call" | custom-call | tf_op jit(solution)/shard_map/comm/pallas_call | solution.py:548
  33.6 4.3 %windows.1 = (f32[256,1024]{1,0:T(8,128)}, f32[256,1024]{1,0:T(8,128)}) custom-call(f32[304,1152]{1,0:T(8,128)S(1)} %get-tuple-element.4.normed_ref, f32[9,128]{1,0:T(8,128)S(1)} %get-tuple-element.5.factor_ref), custom_call_target="tpu_custom_call" | custom-call | tf_op jit(solution)/shard_map/windows/pallas_call | solution.py:517

commit v9 on v8

--- a/solution.py
+++ b/solution.py
@@ -72,6 +72,8 @@
             return (lax.rem(pos + first + steps[slot] + n_pos, n_pos), there)
         return (at_pos((0, -1, 1)[slot - n_steps]), there)
 
+    meets = pos + first + steps[0] < n_pos
+
     def within(place):
         return (place >= 0) & (place < n_pos)
 
@@ -80,13 +82,14 @@
         if slot < n_steps:
             valid = within(pos - ratio * there - steps[slot])
             return valid & (off > 0) if t == 0 and slot == self_step else valid
-        return within(pos + (0, 1, -1)[slot - n_steps])
+        to = pos + (0, 1, -1)[slot - n_steps]
+        return within(to) & (to + ratio * there + steps[0] < n_pos)
 
     def wts_receives(t, slot):
         if slot < n_steps:
             valid = within(pos + first + steps[slot])
             return valid & (off > 0) if t == 0 and slot == self_step else valid
-        return within(pos + (0, -1, 1)[slot - n_steps])
+        return within(pos + (0, -1, 1)[slot - n_steps]) & meets
 
     moves = []
     for t in list(range(1, far_offs)) + [0]:
@@ -109,10 +112,7 @@
         pl.semaphore_signal(barrier, inc=1, device_id=device, device_id_type=MESH)
 
     for t, slot in moves:
-        if slot == own_slot:
-            greet(wts_source(t, slot))
-        else:
-            pl.when(wts_receives(t, slot))(functools.partial(greet, wts_source(t, slot)))
+        pl.when(wts_receives(t, slot))(functools.partial(greet, wts_source(t, slot)))
     for device in cov_peers:
         greet(device)
     for a, b in halo_moves:
@@ -251,10 +251,7 @@
         for (t, slot), copy in zip(moves, wts_copies):
             if side != (slot > own_slot):
                 continue
-            if slot == own_slot:
-                getattr(copy, act)()
-            else:
-                pl.when(valid(t, slot))(getattr(copy, act))
+            pl.when(valid(t, slot))(getattr(copy, act))
 
     each_wts("start", False)
     wts[0, own_slot] = own[...]
@@ -342,7 +339,7 @@
     each_wts("wait_recv", False)
     weigh(0, own_slot + 1)
     for h in range(row_halves):
-        row_w[TOP + h * LANE : TOP + (h + 1) * LANE, :] = down(lines[own_slot, h : h + 1, :])
+        row_w[TOP + h * LANE : TOP + (h + 1) * LANE, :] = down(jnp.where(meets, lines[own_slot, h : h + 1, :], 0.0))
     spread(lines)
 
     def row_group(g):
@@ -385,7 +382,7 @@
     for side, h, low, place in ((0, row_halves - 1, LANE - TOP, 0), (1, 0, 0, TOP + rows)):
         block = pos + (1 if side else -1)
         inside = (block >= 0) & (block < n_pos)
-        weight = jnp.where(inside, lines[own_slot + 1 + side, h : h + 1, :], 0.0)
+        weight = jnp.where(inside & meets, lines[own_slot + 1 + side, h : h + 1, :], 0.0)
         row_w[place : place + TOP, :] = down(weight)[low : low + TOP, :]
     for g in list(range(TOP // 8)) + list(range((TOP + rows) // 8, (2 * TOP + rows) // 8)):
         row_group(g)

time: 38 us -> 38 us (level)
  no operation moved by 1% of the time
where the time goes in v9:
time: 38 us; the launch traced here: 37.9 us
  Pallas kernels  37.2 us (98%)
  between operations  0.64 us (2%)
    pallas_call x1, Pallas kernels, local(): pl.pallas_call(functools.partial(comm_kernel, (n_pos, n_off)), out_shape=...  33 us
    pallas_call x1, Pallas kernels, windows(): pl.pallas_call(window_kernel, out_shape=(out, out), in_specs=[pl.BlockSpe...  4.25 us

profile of v9, /device:TPU:1, one launch (start us, length us, event | category | flops | bytes accessed | tf_op | source)
XLA Modules:
  0.0 37.9 jit_solution(4344647015734715985)
XLA Ops:
  0.6 33.0 %comm.1 = (f32[304,1152]{1,0:T(8,128)S(1)}, f32[9,128]{1,0:T(8,128)S(1)}) custom-call(f32[256,1024]{1,0:T(8,128)} %counts_ref.1, s32[2,128]{1,0:T(2,128)} %bitcast.1), custom_call_target="tpu_custom_call" | custom-call | tf_op jit(solution)/shard_map/comm/pallas_call | solution.py:545
  33.6 4.3 %windows.1 = (f32[256,1024]{1,0:T(8,128)}, f32[256,1024]{1,0:T(8,128)}) custom-call(f32[304,1152]{1,0:T(8,128)S(1)} %get-tuple-element.4.normed_ref, f32[9,128]{1,0:T(8,128)S(1)} %get-tuple-element.5.factor_ref), custom_call_target="tpu_custom_call" | custom-call | tf_op jit(solution)/shard_map/windows/pallas_call | solution.py:514

commit v10 on v9

--- a/solution.py
+++ b/solution.py
@@ -51,6 +51,13 @@
     quot = pos // inner
     rank = pos - quot * inner
     cov_peers = [(pos, far * near_offs + lax.rem(near + r, near_offs)) for r in range(1, near_offs)]
+
+    def cov_source(r):
+        return far * near_offs + lax.rem(near - r + near_offs, near_offs)
+
+    def counts_of(r):
+        return pos + ratio * cov_source(r) < n_pos
+
     halo_moves = [(0, -1), (0, 1), (-1, 0), (1, 0), (-1, -1), (-1, 1), (1, -1), (1, 1)]
     steps = list(range(-1, ratio + 2))
     n_steps = len(steps)
@@ -113,8 +120,8 @@
 
     for t, slot in moves:
         pl.when(wts_receives(t, slot))(functools.partial(greet, wts_source(t, slot)))
-    for device in cov_peers:
-        greet(device)
+    for r in range(1, near_offs):
+        pl.when(counts_of(r))(functools.partial(greet, (pos, cov_source(r))))
     for a, b in halo_moves:
         source = (at_pos(-a), at_off(-b))
         if b == 0:
@@ -152,7 +159,7 @@
     load_mask.wait()
     own_live[...] = mask[...].astype(jnp.float32)
 
-    n_greet = len(cov_peers) + len(part_peers) + len(group_peers)
+    n_greet = len(part_peers) + len(group_peers) + jnp.where(pos + first < n_pos, len(cov_peers), 0)
     for _, b in halo_moves:
         n_greet = n_greet + (jnp.where(sends(b), 1, 0) if b else 1)
     for t, slot in moves:
@@ -168,7 +175,7 @@
         remote(cov.at[0], cov.at[r], cov_send.at[r], cov_recv.at[r], cov_peers[r - 1]) for r in range(1, near_offs)
     ]
     for copy in cov_copies:
-        copy.start()
+        pl.when(pos + first < n_pos)(copy.start)
 
     live_copies = [
         remote(own_live, live.at[k], live_send.at[k], live_recv.at[k], wts_target(0, k)) for k in live_slots
@@ -234,11 +241,11 @@
 
     each_halo(halos[:2], "start")
 
-    for copy in cov_copies:
-        copy.wait_recv()
+    for r, copy in enumerate(cov_copies, 1):
+        pl.when(counts_of(r))(copy.wait_recv)
     coverage = cov[0]
     for r in range(1, near_offs):
-        coverage = coverage + cov[r]
+        coverage = coverage + jnp.where(counts_of(r), cov[r], 0.0)
     own[...] = coverage
 
     wts_copies = [
@@ -387,7 +394,9 @@
     for g in list(range(TOP // 8)) + list(range((TOP + rows) // 8, (2 * TOP + rows) // 8)):
         row_group(g)
 
-    for copy in cov_copies + part_copies + part_live_copies:
+    for copy in cov_copies:
+        pl.when(pos + first < n_pos)(copy.wait_send)
+    for copy in part_copies + part_live_copies:
         copy.wait_send()
     each_halo(halos, "wait_send")
     each_wts("wait_send", False)

time: 38 us -> 38.2 us (level)
  no operation moved by 1% of the time
where the time goes in v10:
time: 38.2 us; the launch traced here: 38.1 us
  Pallas kernels  37.4 us (98%)
  between operations  0.64 us (2%)
    pallas_call x1, Pallas kernels, local(): pl.pallas_call(functools.partial(comm_kernel, (n_pos, n_off)), out_shape=...  33.2 us
    pallas_call x1, Pallas kernels, windows(): pl.pallas_call(window_kernel, out_shape=(out, out), in_specs=[pl.BlockSpe...  4.26 us

profile of v10, /device:TPU:1, one launch (start us, length us, event | category | flops | bytes accessed | tf_op | source)
XLA Modules:
  0.0 38.1 jit_solution(16602923327235222011)
XLA Ops:
  0.6 33.2 %comm.1 = (f32[304,1152]{1,0:T(8,128)S(1)}, f32[9,128]{1,0:T(8,128)S(1)}) custom-call(f32[256,1024]{1,0:T(8,128)} %counts_ref.1, s32[2,128]{1,0:T(2,128)} %bitcast.1), custom_call_target="tpu_custom_call" | custom-call | tf_op jit(solution)/shard_map/comm/pallas_call | solution.py:554
  33.8 4.3 %windows.1 = (f32[256,1024]{1,0:T(8,128)}, f32[256,1024]{1,0:T(8,128)}) custom-call(f32[304,1152]{1,0:T(8,128)S(1)} %get-tuple-element.4.normed_ref, f32[9,128]{1,0:T(8,128)S(1)} %get-tuple-element.5.factor_ref), custom_call_target="tpu_custom_call" | custom-call | tf_op jit(solution)/shard_map/windows/pallas_call | solution.py:523

commit v11 on v9

--- a/solution.py
+++ b/solution.py
@@ -455,7 +455,7 @@
     pair_table, last_table = [], []
     for k in (0, 2):
         pair_table.append(jnp.concatenate([main_t[k]] * 2 + [main_t[k + 1]] * 2 + [rim_t[k]] * 2 + [rim_t[k + 1]] * 2, axis=0))
-        last_table.append(jnp.concatenate([mid_t[k], edge_t[k]] * 2 + [mid_t[k + 1], edge_t[k + 1]] * 2, axis=0))
+        last_table.append(jnp.concatenate([mid_t[k], edge_t[k], mid_t[k + 1], edge_t[k + 1]], axis=0))
     flip = 7 - lax.broadcasted_iota(jnp.int32, (8, cols), 0)
     cells_donut = (2 * W + 1) ** 2 - (2 * P_SIZE + 1) ** 2 - 4 * (W - P_SIZE)
     cells_lower = W * W - P_SIZE * P_SIZE
@@ -491,7 +491,12 @@
         ):
             (m0, r0, l0), (m1, r1, l1) = sideways(summed, k), sideways(summed, k + 1)
             tall = jnp.dot(jnp.concatenate(m0 + m1 + r0 + r1, axis=1), pair_table[k // 2], preferred_element_type=jnp.float32)
-            end = jnp.dot(jnp.concatenate(l0 + l1, axis=1), last_table[k // 2], preferred_element_type=jnp.float32)
+            end = jnp.dot(
+                jnp.concatenate([jnp.concatenate([l0[n], l1[n]], axis=1) for n in (0, 1)], axis=0),
+                last_table[k // 2],
+                preferred_element_type=jnp.float32,
+            )
+            end = end[:STEP] + end[STEP:]
             flat = jnp.concatenate([tall[c * STEP : (c + 1) * STEP, :] for c in range(blocks // 2)] + [end], axis=1)
             for g in range(STEP // 8):
                 rows_g = slice(8 * g, 8 * g + 8)

time: 38 us -> 38 us (level)
  no operation moved by 1% of the time
where the time goes in v11:
time: 38 us; the launch traced here: 37.8 us
  Pallas kernels  37.2 us (98%)
  between operations  0.64 us (2%)
    pallas_call x1, Pallas kernels, local(): pl.pallas_call(functools.partial(comm_kernel, (n_pos, n_off)), out_shape=...  33 us
    pallas_call x1, Pallas kernels, windows(): pl.pallas_call(window_kernel, out_shape=(out, out), in_specs=[pl.BlockSpe...  4.21 us

profile of v11, /device:TPU:1, one launch (start us, length us, event | category | flops | bytes accessed | tf_op | source)
XLA Modules:
  0.0 37.8 jit_solution(16716807409394314630)
XLA Ops:
  0.6 33.0 %comm.1 = (f32[304,1152]{1,0:T(8,128)S(1)}, f32[9,128]{1,0:T(8,128)S(1)}) custom-call(f32[256,1024]{1,0:T(8,128)} %counts_ref.1, s32[2,128]{1,0:T(2,128)} %bitcast.1), custom_call_target="tpu_custom_call" | custom-call | tf_op jit(solution)/shard_map/comm/pallas_call | solution.py:550
  33.6 4.2 %windows.1 = (f32[256,1024]{1,0:T(8,128)}, f32[256,1024]{1,0:T(8,128)}) custom-call(f32[304,1152]{1,0:T(8,128)S(1)} %get-tuple-element.4.normed_ref, f32[9,128]{1,0:T(8,128)S(1)} %get-tuple-element.5.factor_ref), custom_call_target="tpu_custom_call" | custom-call | tf_op jit(solution)/shard_map/windows/pallas_call | solution.py:519
